TPU v7x, 32 devices: a whole 2x2x4 slice. The times are simulated.
32 devices in a mesh: sec: 4 (over y, x), vel: 8 (over z, core).
Axes of the slice: x: 2, y: 2, z: 4, core: 2. Of those that a mesh axis runs over, the one named last changes fastest.
Arguments:
- distribution: float32 [13824, 1024], P('vel', 'sec'), may hold values from -6 to 6
- collision: float32 [1024], P('sec'), may hold values from 0.05 to 2
- lower_blocks: float32 [25, 1024], P(None, 'sec'), may hold values from -0.6 to 0.6
- upper_blocks: float32 [25, 1024], P(None, 'sec'), may hold values from -0.6 to 0.6
- diag_inverse: float32 [25, 1024], P(None, 'sec'), may hold values from -0.2 to 1.4
Outputs:
- new_distribution: float32 [13824, 1024], P('vel', 'sec')
- macro: float32 [5, 1024], P(None, 'sec')
All inputs are finite; a program needn't handle non-finite values.
Results may differ from a plain program's by a relative error of at most 0.0003.
Values sent between devices are 32-bit elements; how exact they have to be, the bound alone decides.
A program may use at most 64 MiB of HBM per device.

v0:
```python
import math

import jax
import jax.numpy as jnp
import numpy as np
from jax import lax
from jax.sharding import PartitionSpec as P

NXI = 24
TUBES = 128
JACOBI = 4
NEWTON = 2


HIGH = lax.Precision.HIGHEST
pseudo_rate = 1.0


def passed_along(block, axis, distance):
    devices = range(lax.axis_size(axis))
    route = [(i - distance, i) for i in devices if i - distance in devices]
    return lax.ppermute(block, axis, route)


def extended(array, sides, width):
    for axis, dim in sides:
        count, length = (lax.axis_size(axis), array.shape[dim])
        up = [(i, (i + 1) % count) for i in range(count - 1)]
        down = [(j, i) for i, j in up]
        last = lax.slice_in_dim(array, length - width, length, axis=dim)
        first = lax.slice_in_dim(array, 0, width, axis=dim)
        before = lax.ppermute(last, axis, up)
        after = lax.ppermute(first, axis, down)
        array = jnp.concatenate([before, array, after], axis=dim)
    return array


def hermite_rule(count):
    quarter = math.pi ** (-0.25)
    found = []
    last_slope = 1.0
    for index in range(count // 2):
        if index == 0:
            guess = math.sqrt(2.0 * count + 1.0) - 1.85575 * (2.0 * count + 1.0) ** (-0.16667)
        elif index == 1:
            guess = guess - 1.14 * count**0.426 / guess
        elif index == 2:
            guess = 1.86 * guess - 0.86 * found[0][0]
        elif index == 3:
            guess = 1.91 * guess - 0.91 * found[1][0]
        else:
            guess = 2.0 * guess - found[index - 2][0]
        for repeat in range(60):
            current = quarter
            previous = 0.0
            for order in range(count):
                older = previous
                previous = current
                current = (
                    guess * math.sqrt(2.0 / (order + 1)) * previous
                    - math.sqrt(order / (order + 1.0)) * older
                )
            last_slope = math.sqrt(2.0 * count) * previous
            guess = guess - current / last_slope
        found.append((guess, 2.0 / (last_slope * last_slope)))
    positive = found[::-1]
    points = [-pair[0] for pair in found] + [pair[0] for pair in positive]
    weights = [pair[1] for pair in found] + [pair[1] for pair in positive]
    return (np.array(points), np.array(weights))


def node_tables(axis_points):
    points, weights = hermite_rule(axis_points)
    node_index = np.arange(axis_points**3)
    idx_x = node_index % axis_points
    idx_z = node_index // axis_points % axis_points
    idx_y = node_index // (axis_points * axis_points)
    along_x = points[idx_x]
    along_y = points[idx_y]
    along_z = points[idx_z]
    node_weight = weights[idx_x] * weights[idx_y] * weights[idx_z] / math.pi**1.5
    energy = along_x**2 + along_y**2 + along_z**2 - 1.5
    moment_basis = np.stack([along_x * 0.0 + 1.0, along_x, along_y, along_z, energy])
    norm_scale = np.array([1.0, 0.5, 0.5, 0.5, 1.5])
    return (
        along_x,
        node_weight,
        moment_basis * node_weight[None, :],
        moment_basis / norm_scale[:, None],
    )


def apply_block(matrices, vector):
    shaped = matrices.reshape((5, 5) + vector.shape[1:])
    return jnp.sum(shaped * vector[None], axis=1)


def affine_combine(earlier_map, later_map):
    return (later_map[0] * earlier_map[0], later_map[0] * earlier_map[1] + later_map[1])


def newton_sums(loaded, signed, shift_mass, shift_flow):
    growth = jnp.exp(shift_mass + shift_flow * signed)
    scaled = loaded * growth
    excess = loaded * (growth - 1.0)
    return jnp.stack(
        [
            jnp.sum(scaled),
            jnp.sum(scaled * signed),
            jnp.sum(scaled * signed * signed),
            jnp.sum(excess),
            jnp.sum(excess * signed),
        ]
    )


def newton_update(shift_mass, shift_flow, sums, goal_mass, goal_flow):
    resid_mass = sums[3] - goal_mass
    resid_flow = sums[4] - goal_flow
    determinant = sums[0] * sums[2] - sums[1] * sums[1]
    new_mass = shift_mass - (sums[2] * resid_mass - sums[1] * resid_flow) / determinant
    new_flow = shift_flow - (sums[0] * resid_flow - sums[1] * resid_mass) / determinant
    return (new_mass, new_flow)


def body(distribution, collision, lower_blocks, upper_blocks, diag_inverse):
    node_count = distribution.shape[0]
    cell_count = distribution.shape[1]
    length = cell_count // TUBES
    node_rows = node_count // NXI
    half_nodes = NXI // 2
    along_x, node_weight, weighted_np, rebuild_np = node_tables(NXI)
    all_signed = jnp.asarray(along_x, jnp.float32)
    all_mass = jnp.asarray(node_weight, jnp.float32)
    offset = lax.axis_index("vel") * node_count
    weighted = lax.dynamic_slice_in_dim(
        jnp.asarray(weighted_np, jnp.float32), offset, node_count, 1
    )
    rebuild = lax.dynamic_slice_in_dim(jnp.asarray(rebuild_np, jnp.float32), offset, node_count, 1)
    signed = lax.dynamic_slice_in_dim(all_signed, offset, node_count, 0)
    old_moments = lax.psum(jnp.dot(weighted, distribution, precision=HIGH), "vel")
    target = jnp.dot(rebuild.T, old_moments, precision=HIGH)
    total_length = length * lax.axis_size("sec")
    thickness = collision.reshape(1, 1, length, TUBES)
    node_speed = jnp.abs(signed).reshape(node_rows, NXI, 1, 1)
    denominator = node_speed * total_length + thickness + pseudo_rate
    carry_rate = node_speed * total_length / denominator
    drive_term = (
        thickness * target.reshape(node_rows, NXI, length, TUBES)
        + pseudo_rate * distribution.reshape(node_rows, NXI, length, TUBES)
    ) / denominator
    prod_neg, local_neg = lax.associative_scan(
        affine_combine,
        (carry_rate[:, :half_nodes], drive_term[:, :half_nodes]),
        reverse=True,
        axis=2,
    )
    prod_pos, local_pos = lax.associative_scan(
        affine_combine, (carry_rate[:, half_nodes:], drive_term[:, half_nodes:]), axis=2
    )
    summary_pos = (prod_pos[:, :, -1], local_pos[:, :, -1])
    summary_neg = (prod_neg[:, :, 0], local_neg[:, :, 0])

    def relay(turn_index, inflows):
        out_pos = summary_pos[0] * inflows[0] + summary_pos[1]
        out_neg = summary_neg[0] * inflows[1] + summary_neg[1]
        return (passed_along(out_pos, "sec", 1), passed_along(out_neg, "sec", -1))

    start_flows = (jnp.zeros_like(summary_pos[1]), jnp.zeros_like(summary_neg[1]))
    inflow_pos, inflow_neg = lax.fori_loop(0, lax.axis_size("sec") - 1, relay, start_flows)
    field_neg = local_neg + prod_neg * inflow_neg[:, :, None, :]
    field_pos = local_pos + prod_pos * inflow_pos[:, :, None, :]
    half_field = jnp.concatenate([field_neg, field_pos], axis=1).reshape(node_count, cell_count)
    half_moments = lax.psum(jnp.dot(weighted, half_field, precision=HIGH), "vel")
    residual = (half_moments - old_moments).reshape(5, length, TUBES)
    lower_r = lower_blocks.reshape(25, length, TUBES)
    upper_r = upper_blocks.reshape(25, length, TUBES)
    inverse_r = diag_inverse.reshape(25, length, TUBES)
    correction = apply_block(inverse_r, residual)
    for sweep_index in range(JACOBI):
        padded = extended(correction, (("sec", 1),), 1)
        correction = apply_block(
            inverse_r,
            residual - apply_block(lower_r, padded[:, :-2]) - apply_block(upper_r, padded[:, 2:]),
        )
    correction = correction.reshape(5, cell_count)
    macro = half_moments + correction
    synthetic = half_field + jnp.dot(rebuild.T, correction, precision=HIGH)
    local_totals = jnp.sum(old_moments - macro, axis=1)[0:2]
    magnitude = jnp.sum(jnp.abs(synthetic), axis=1)
    shift_mass = jnp.zeros((), jnp.float32)
    shift_flow = jnp.zeros((), jnp.float32)
    node_total, goals = lax.psum((magnitude, local_totals), "sec")
    every_node = lax.all_gather(node_total, "vel", axis=0, tiled=True)
    loaded = all_mass * every_node
    for newton_turn in range(NEWTON):
        sums = newton_sums(loaded, all_signed, shift_mass, shift_flow)
        shift_mass, shift_flow = newton_update(shift_mass, shift_flow, sums, goals[0], goals[1])
    growth = jnp.exp(shift_mass + shift_flow * signed)
    new_distribution = synthetic + jnp.abs(synthetic) * (growth[:, None] - 1.0)
    return (new_distribution, macro)


def solution(mesh):
    in_specs = (P("vel", "sec"), P("sec"), P(None, "sec"), P(None, "sec"), P(None, "sec"))
    out_specs = (P("vel", "sec"), P(None, "sec"))
    return jax.shard_map(body, mesh=mesh, in_specs=in_specs, out_specs=out_specs, check_vma=False)
```

profile of v0, /device:TPU:0, one launch (start us, length us, event | category | flops | bytes accessed | tf_op | source)
XLA Modules:
  0.0 232.2 jit_solution(7167413531057420676)
XLA Ops:
  0.6 2.3 reshape.85
  2.9 1.7 fusion.12
  4.6 18.3 %psum.28 = f32[5,256]{1,0:T(8,128)S(1)} all-reduce(f32[5,256]{1,0:T(8,128)S(1)} %fusion.12), channel_id=1, replica_groups=mesh['sec'=4,'vel'=8] {'vel'}, use_global_device_ids=true, to_apply=%region_0.0 | all-reduce | flops 1280 | bytes 10240 | tf_op jit(solution)/shard_map/psum | solution.py:141
  23.0 3.8 %fusion.15 = f32[1728,256]{1,0:T(8,128)} fusion(f32[5,256]{1,0:T(8,128)S(1)} %psum.28, f32[5,13824]{1,0:T(8,128)} %constant.39.clone, s32[]{:T(128)S(6)} %select_n.2), kind=kOutput, calls=%fused_computation.43 | convolution fusion | flops 26542080 | bytes 1831940 | tf_op jit(solution)/shard_map/dot_general | solution.py:142
  26.8 2.1 reshape.84
  30.4 3.8 %fusion.3 = (f32[72,24,2,128]{3,2,1,0:T(2,128)S(1)}, f32[72,24,2,128]{3,2,1,0:T(2,128)S(1)}) fusion(f32[72,24,2,128]{3,2,1,0:T(2,128)S(1)} %reshape.85, f32[72,24,2,128]{3,2,1,0:T(2,128)S(1)} %reshape.84, f32[72,24]{1,0:T(8,128)} %mul.265, f32[2,128]{1,0:T(2,128)} %bitcast.42), kind=kLoop, calls=%fused_computation.9 | loop fusion | flops 2654208 | bytes 7085824 | tf_op jit(solution)/shard_map/div | solution.py:148
  34.2 2.7 %slice_add_fusion.1 = (f32[72,12,1,128]{3,2,1,0:T(1,128)S(1)}, f32[72,12,1,128]{3,2,1,0:T(1,128)S(1)}, f32[72,12,1,128]{3,2,1,0:T(1,128)S(1)}, f32[72,12,1,128]{...) fusion(f32[72,24,2,128]{3,2,1,0:T(2,128)S(1)} %get-tuple-elemen, ...), kind=kLoop, calls=%fused_computation.32 | loop fusion | flops 663552 | bytes 7077888 | tf_op jit(solution)/shard_map/add | solution.py:99
  38.4 2.3 fusion.7
  40.7 4.9 %rev.8 = f32[72,12,2,128]{3,2,1,0:T(2,128)} reverse(f32[72,12,2,128]{3,2,1,0:T(2,128)S(1)} %get-tuple-element.113), dimensions={2} | reverse | bytes 1769472 | tf_op jit(solution)/shard_map/rev | solution.py:152
  45.6 5.0 %rev.9 = f32[72,12,2,128]{3,2,1,0:T(2,128)} reverse(f32[72,12,2,128]{3,2,1,0:T(2,128)S(1)} %get-tuple-element.112), dimensions={2} | reverse | bytes 1769472 | tf_op jit(solution)/shard_map/rev | solution.py:152
  52.4 59.8 %while.12 = (s32[]{:T(128)}, f32[72,12,128]{2,0,1:T(8,128)S(1)}, f32[72,12,128]{2,0,1:T(8,128)S(1)}, f32[72,12,128]{2,0,1:T(8,128)S(1)}, f32[72,12,128]{2,0,1:T(...) while((s32[]{:T(128)}, f32[72,12,128]{2,0,1:T(8,128)S(1)}, ...), condition=%wide.region_2.0_spmd, body=%wide.region_1.0_spmd.sunk | while | flops 442370 | bytes 7078053 | solution.py:170
  52.5 3.4 %collective-permute-start = (f32[72,12,128]{2,0,1:T(8,128)S(1)}, f32[72,12,128]{2,0,1:T(8,128)S(1)}, u32[]{:S(2)}, u32[]{:S(2)}) collective-permute-start(f32[72,12,128]{2,0,1:T(8,128)S(1)} %multiply_add_fusion.6), channel_id=1, source_target_pairs={{0,8},{8,16},{16,24},{1,9},{9,17},{17,25},{2,10},{10,18},{18,26},{... | collective-permute-start | bytes 1327112 | tf_op jit(solution)/shard_map/while/body/eval_jaxpr/ppermute | solution.py:22
  57.3 5.2 %collective-permute-done = f32[72,12,128]{2,0,1:T(8,128)S(1)} collective-permute-done((f32[72,12,128]{2,0,1:T(8,128)S(1)}, f32[72,12,128]{2,0,1:T(8,128)S(1)}, u32[]{:S(2)}, u32[]{:S(2)}) %collective-permute-start) | collective-permute-done | bytes 442400 | tf_op jit(solution)/shard_map/while/body/eval_jaxpr/ppermute | solution.py:22
  62.4 11.4 %collective-permute-done.1 = f32[72,12,128]{2,0,1:T(8,128)S(1)} collective-permute-done((f32[72,12,128]{2,0,1:T(8,128)S(1)}, f32[72,12,128]{2,0,1:T(8,128)S(1)}, u32[]{:S(2)}, u32[]{:S(2)}) %collective-permute-start.1) | collective-permute-done | bytes 442400 | tf_op jit(solution)/shard_map/while/body/eval_jaxpr/ppermute | solution.py:22
  73.9 4.9 %collective-permute-start = (f32[72,12,128]{2,0,1:T(8,128)S(1)}, f32[72,12,128]{2,0,1:T(8,128)S(1)}, u32[]{:S(2)}, u32[]{:S(2)}) collective-permute-start(f32[72,12,128]{2,0,1:T(8,128)S(1)} %multiply_add_fusion.6), channel_id=1, source_target_pairs={{0,8},{8,16},{16,24},{1,9},{9,17},{17,25},{2,10},{10,18},{18,26},{... | collective-permute-start | bytes 1327112 | tf_op jit(solution)/shard_map/while/body/eval_jaxpr/ppermute | solution.py:22
  80.2 4.4 %collective-permute-done = f32[72,12,128]{2,0,1:T(8,128)S(1)} collective-permute-done((f32[72,12,128]{2,0,1:T(8,128)S(1)}, f32[72,12,128]{2,0,1:T(8,128)S(1)}, u32[]{:S(2)}, u32[]{:S(2)}) %collective-permute-start) | collective-permute-done | bytes 442400 | tf_op jit(solution)/shard_map/while/body/eval_jaxpr/ppermute | solution.py:22
  84.6 9.0 %collective-permute-done.1 = f32[72,12,128]{2,0,1:T(8,128)S(1)} collective-permute-done((f32[72,12,128]{2,0,1:T(8,128)S(1)}, f32[72,12,128]{2,0,1:T(8,128)S(1)}, u32[]{:S(2)}, u32[]{:S(2)}) %collective-permute-start.1) | collective-permute-done | bytes 442400 | tf_op jit(solution)/shard_map/while/body/eval_jaxpr/ppermute | solution.py:22
  93.7 4.6 %collective-permute-start = (f32[72,12,128]{2,0,1:T(8,128)S(1)}, f32[72,12,128]{2,0,1:T(8,128)S(1)}, u32[]{:S(2)}, u32[]{:S(2)}) collective-permute-start(f32[72,12,128]{2,0,1:T(8,128)S(1)} %multiply_add_fusion.6), channel_id=1, source_target_pairs={{0,8},{8,16},{16,24},{1,9},{9,17},{17,25},{2,10},{10,18},{18,26},{... | collective-permute-start | bytes 1327112 | tf_op jit(solution)/shard_map/while/body/eval_jaxpr/ppermute | solution.py:22
  99.8 4.4 %collective-permute-done = f32[72,12,128]{2,0,1:T(8,128)S(1)} collective-permute-done((f32[72,12,128]{2,0,1:T(8,128)S(1)}, f32[72,12,128]{2,0,1:T(8,128)S(1)}, u32[]{:S(2)}, u32[]{:S(2)}) %collective-permute-start) | collective-permute-done | bytes 442400 | tf_op jit(solution)/shard_map/while/body/eval_jaxpr/ppermute | solution.py:22
  104.2 8.0 %collective-permute-done.1 = f32[72,12,128]{2,0,1:T(8,128)S(1)} collective-permute-done((f32[72,12,128]{2,0,1:T(8,128)S(1)}, f32[72,12,128]{2,0,1:T(8,128)S(1)}, u32[]{:S(2)}, u32[]{:S(2)}) %collective-permute-start.1) | collective-permute-done | bytes 442400 | tf_op jit(solution)/shard_map/while/body/eval_jaxpr/ppermute | solution.py:22
  116.5 1.7 fusion
  118.2 21.3 %psum.29 = f32[5,256]{1,0:T(8,128)S(1)} all-reduce(f32[5,256]{1,0:T(8,128)S(1)} %fusion), channel_id=1, replica_groups=mesh['sec'=4,'vel'=8] {'vel'}, use_global_device_ids=true, to_apply=%region_3.0 | all-reduce | flops 1280 | bytes 10240 | tf_op jit(solution)/shard_map/psum | solution.py:174
  142.5 4.1 %collective-permute-done.3 = f32[5,1,128]{2,1,0:T(1,128)S(1)} collective-permute-done((f32[5,1,128]{2,1,0:T(1,128)S(1)}, f32[5,1,128]{2,1,0:T(1,128)S(1)}, u32[]{:S(2)}, u32[]{:S(2)}) %collective-permute-start.3) | collective-permute-done | bytes 2592 | tf_op jit(solution)/shard_map/ppermute | solution.py:33
  146.7 2.8 %collective-permute-start.4 = (f32[5,1,128]{2,1,0:T(1,128)S(1)}, f32[5,1,128]{2,1,0:T(1,128)S(1)}, u32[]{:S(2)}, u32[]{:S(2)}) collective-permute-start(f32[5,1,128]{2,1,0:T(1,128)S(1)} %get-tuple-element.102), channel_id=1, source_target_pairs={{0,8},{8,16},{16,24},{1,9},{9,17},{17,25},{2,10},{10,18},{18,26},{... | collective-permute-start | bytes 7688 | tf_op jit(solution)/shard_map/ppermute | solution.py:32
  150.8 4.2 %collective-permute-done.5 = f32[5,1,128]{2,1,0:T(1,128)S(1)} collective-permute-done((f32[5,1,128]{2,1,0:T(1,128)S(1)}, f32[5,1,128]{2,1,0:T(1,128)S(1)}, u32[]{:S(2)}, u32[]{:S(2)}) %collective-permute-start.5) | collective-permute-done | bytes 2592 | tf_op jit(solution)/shard_map/ppermute | solution.py:33
  155.1 2.8 %collective-permute-start.6 = (f32[5,1,128]{2,1,0:T(1,128)S(1)}, f32[5,1,128]{2,1,0:T(1,128)S(1)}, u32[]{:S(2)}, u32[]{:S(2)}) collective-permute-start(f32[5,1,128]{2,1,0:T(1,128)S(1)} %get-tuple-element.98), channel_id=1, source_target_pairs={{0,8},{8,16},{16,24},{1,9},{9,17},{17,25},{2,10},{10,18},{18,26},{... | collective-permute-start | bytes 7688 | tf_op jit(solution)/shard_map/ppermute | solution.py:32
  159.3 4.2 %collective-permute-done.7 = f32[5,1,128]{2,1,0:T(1,128)S(1)} collective-permute-done((f32[5,1,128]{2,1,0:T(1,128)S(1)}, f32[5,1,128]{2,1,0:T(1,128)S(1)}, u32[]{:S(2)}, u32[]{:S(2)}) %collective-permute-start.7) | collective-permute-done | bytes 2592 | tf_op jit(solution)/shard_map/ppermute | solution.py:33
  163.6 2.8 %collective-permute-start.8 = (f32[5,1,128]{2,1,0:T(1,128)S(1)}, f32[5,1,128]{2,1,0:T(1,128)S(1)}, u32[]{:S(2)}, u32[]{:S(2)}) collective-permute-start(f32[5,1,128]{2,1,0:T(1,128)S(1)} %get-tuple-element.94), channel_id=1, source_target_pairs={{0,8},{8,16},{16,24},{1,9},{9,17},{17,25},{2,10},{10,18},{18,26},{... | collective-permute-start | bytes 7688 | tf_op jit(solution)/shard_map/ppermute | solution.py:32
  169.2 2.7 %collective-permute-done.9 = f32[5,1,128]{2,1,0:T(1,128)S(1)} collective-permute-done((f32[5,1,128]{2,1,0:T(1,128)S(1)}, f32[5,1,128]{2,1,0:T(1,128)S(1)}, u32[]{:S(2)}, u32[]{:S(2)}) %collective-permute-start.9) | collective-permute-done | bytes 2592 | tf_op jit(solution)/shard_map/ppermute | solution.py:33
  172.7 2.8 %abs_reduce_fusion = (f32[1728]{0:T(1024)S(1)}, f32[1728,256]{1,0:T(8,128)S(1)}) fusion(f32[1,5,2,128]{3,2,1,0:T(2,128)S(1)} %bitcast.40, f32[5,13824]{1,0:T(8,128)} %constant.39.clone, s32[]{:T(128)S(6)} %select_n.2, f32[216,8,2,128]{3,2,1,0:T(2,128)S(1)} %bitcast.38), kind=kOutput, calls=%fused_computation.11 | convolution fusion | flops 27867456 | bytes 3608324 | tf_op jit(solution)/shard_map/dot_general | solution.py:188
  175.5 8.7 %all-reduce.9 = (f32[1728]{0:T(1024)S(1)}, f32[2]{0:T(128)S(1)}) all-reduce(f32[1728]{0:T(1024)S(1)} %get-tuple-element.110, f32[2]{0:T(128)S(1)} %bitcast.41), channel_id=1, replica_groups=mesh['sec'=4,'vel'=8] {'sec'}, use_global_device_ids=true, to_apply=%region_18.0 | all-reduce | flops 1730 | bytes 13840 | tf_op jit(solution)/shard_map/psum | solution.py:193
  184.5 26.4 %all-reduce.8 = f32[13824]{0:T(1024)S(1)} all-reduce(f32[13824]{0:T(1024)S(1)} %dynamic-update-slice), channel_id=1, replica_groups=mesh['sec'=4,'vel'=8] {'vel'}, use_global_device_ids=true, to_apply=%add.8 | all-reduce | flops 13824 | bytes 110592
  (106 shorter events, 28.2 us)
Async XLA Ops:
  0.6 2.3 copy-start
  36.9 13.8 %copy-start.1 = (f32[72,12,1,128]{3,2,1,0:T(1,128)}, f32[72,12,1,128]{3,2,1,0:T(1,128)S(1)}, u32[]{:S(2)}) copy-start(f32[72,12,1,128]{3,2,1,0:T(1,128)S(1)} %get-tuple-element.79) | copy-start | bytes 1327108
  36.9 13.8 %copy-start.3 = (f32[72,12,1,128]{3,2,1,0:T(1,128)}, f32[72,12,1,128]{3,2,1,0:T(1,128)S(1)}, u32[]{:S(2)}) copy-start(f32[72,12,1,128]{3,2,1,0:T(1,128)S(1)} %get-tuple-element.81) | copy-start | bytes 1327108
  36.9 13.8 %copy-start.5 = (f32[72,12,1,128]{3,2,1,0:T(1,128)}, f32[72,12,1,128]{3,2,1,0:T(1,128)S(1)}, u32[]{:S(2)}) copy-start(f32[72,12,1,128]{3,2,1,0:T(1,128)S(1)} %get-tuple-element.82) | copy-start | bytes 1327108
  36.9 13.8 %copy-start.7 = (f32[72,12,1,128]{3,2,1,0:T(1,128)}, f32[72,12,1,128]{3,2,1,0:T(1,128)S(1)}, u32[]{:S(2)}) copy-start(f32[72,12,1,128]{3,2,1,0:T(1,128)S(1)} %get-tuple-element.84) | copy-start | bytes 1327108
  45.6 5.0 %copy-start.12 = (f32[72,12,1,128]{3,2,1,0:T(1,128)S(1)}, f32[72,12,1,128]{3,2,1,0:T(1,128)}, u32[]{:S(2)}) copy-start(f32[72,12,1,128]{3,2,1,0:T(1,128)} %get-tuple-element.114) | copy-start | bytes 1327108
  45.6 5.0 %copy-start.11 = (f32[72,12,1,128]{3,2,1,0:T(1,128)S(1)}, f32[72,12,1,128]{3,2,1,0:T(1,128)}, u32[]{:S(2)}) copy-start(f32[72,12,1,128]{3,2,1,0:T(1,128)} %get-tuple-element.115) | copy-start | bytes 1327108
  52.5 10.0 %collective-permute-start = (f32[72,12,128]{2,0,1:T(8,128)S(1)}, f32[72,12,128]{2,0,1:T(8,128)S(1)}, u32[]{:S(2)}, u32[]{:S(2)}) collective-permute-start(f32[72,12,128]{2,0,1:T(8,128)S(1)} %multiply_add_fusion.6), channel_id=1, source_target_pairs={{0,8},{8,16},{16,24},{1,9},{9,17},{17,25},{2,10},{10,18},{18,26},{... | collective-permute-start | bytes 1327112 | tf_op jit(solution)/shard_map/while/body/eval_jaxpr/ppermute | solution.py:22
  56.0 17.9 %collective-permute-start.1 = (f32[72,12,128]{2,0,1:T(8,128)S(1)}, f32[72,12,128]{2,0,1:T(8,128)S(1)}, u32[]{:S(2)}, u32[]{:S(2)}) collective-permute-start(f32[72,12,128]{2,0,1:T(8,128)S(1)} %multiply_add_fusion.7), channel_id=1, source_target_pairs={{8,0},{16,8},{24,16},{9,1},{17,9},{25,17},{10,2},{18,10},{26,18},{... | collective-permute-start | bytes 1327112 | tf_op jit(solution)/shard_map/while/body/eval_jaxpr/ppermute | solution.py:22
  73.9 10.7 %collective-permute-start = (f32[72,12,128]{2,0,1:T(8,128)S(1)}, f32[72,12,128]{2,0,1:T(8,128)S(1)}, u32[]{:S(2)}, u32[]{:S(2)}) collective-permute-start(f32[72,12,128]{2,0,1:T(8,128)S(1)} %multiply_add_fusion.6), channel_id=1, source_target_pairs={{0,8},{8,16},{16,24},{1,9},{9,17},{17,25},{2,10},{10,18},{18,26},{... | collective-permute-start | bytes 1327112 | tf_op jit(solution)/shard_map/while/body/eval_jaxpr/ppermute | solution.py:22
  78.9 14.8 %collective-permute-start.1 = (f32[72,12,128]{2,0,1:T(8,128)S(1)}, f32[72,12,128]{2,0,1:T(8,128)S(1)}, u32[]{:S(2)}, u32[]{:S(2)}) collective-permute-start(f32[72,12,128]{2,0,1:T(8,128)S(1)} %multiply_add_fusion.7), channel_id=1, source_target_pairs={{8,0},{16,8},{24,16},{9,1},{17,9},{25,17},{10,2},{18,10},{26,18},{... | collective-permute-start | bytes 1327112 | tf_op jit(solution)/shard_map/while/body/eval_jaxpr/ppermute | solution.py:22
  93.7 10.4 %collective-permute-start = (f32[72,12,128]{2,0,1:T(8,128)S(1)}, f32[72,12,128]{2,0,1:T(8,128)S(1)}, u32[]{:S(2)}, u32[]{:S(2)}) collective-permute-start(f32[72,12,128]{2,0,1:T(8,128)S(1)} %multiply_add_fusion.6), channel_id=1, source_target_pairs={{0,8},{8,16},{16,24},{1,9},{9,17},{17,25},{2,10},{10,18},{18,26},{... | collective-permute-start | bytes 1327112 | tf_op jit(solution)/shard_map/while/body/eval_jaxpr/ppermute | solution.py:22
  98.5 13.7 %collective-permute-start.1 = (f32[72,12,128]{2,0,1:T(8,128)S(1)}, f32[72,12,128]{2,0,1:T(8,128)S(1)}, u32[]{:S(2)}, u32[]{:S(2)}) collective-permute-start(f32[72,12,128]{2,0,1:T(8,128)S(1)} %multiply_add_fusion.7), channel_id=1, source_target_pairs={{8,0},{16,8},{24,16},{9,1},{17,9},{25,17},{10,2},{18,10},{26,18},{... | collective-permute-start | bytes 1327112 | tf_op jit(solution)/shard_map/while/body/eval_jaxpr/ppermute | solution.py:22
  112.1 1.0 copy-start.2
  112.1 1.1 copy-start.4
  112.1 1.3 copy-start.6
  112.1 1.4 copy-start.8
  113.5 1.5 copy-start.9
  113.5 1.5 copy-start.10
  116.4 23.1 %copy-start.13 = (f32[25,256]{1,0:T(8,128)S(1)}, f32[25,256]{1,0:T(8,128)}, u32[]{:S(2)}) copy-start(f32[25,256]{1,0:T(8,128)} %param.15) | copy-start | bytes 76804
  116.4 25.9 %copy-start.14 = (f32[25,256]{1,0:T(8,128)S(1)}, f32[25,256]{1,0:T(8,128)}, u32[]{:S(2)}) copy-start(f32[25,256]{1,0:T(8,128)} %param.13) | copy-start | bytes 76804
  116.5 26.0 %copy-start.15 = (f32[25,256]{1,0:T(8,128)S(1)}, f32[25,256]{1,0:T(8,128)}, u32[]{:S(2)}) copy-start(f32[25,256]{1,0:T(8,128)} %param.14) | copy-start | bytes 76804
  116.5 51.4 %copy-start.16 = (u32[32]{0:T(128)S(1)}, u32[32]{0:T(128)}, u32[]{:S(2)}) copy-start(u32[32]{0:T(128)} %constant.66) | copy-start | bytes 388
  139.6 2.8 %collective-permute-start.2 = (f32[5,1,128]{2,1,0:T(1,128)S(1)}, f32[5,1,128]{2,1,0:T(1,128)S(1)}, u32[]{:S(2)}, u32[]{:S(2)}) collective-permute-start(f32[5,1,128]{2,1,0:T(1,128)S(1)} %get-tuple-element.106), channel_id=1, source_target_pairs={{0,8},{8,16},{16,24},{1,9},{9,17},{17,25},{2,10},{10,18},{18,26},{... | collective-permute-start | bytes 7688 | tf_op jit(solution)/shard_map/ppermute | solution.py:32
  141.1 5.5 %collective-permute-start.3 = (f32[5,1,128]{2,1,0:T(1,128)S(1)}, f32[5,1,128]{2,1,0:T(1,128)S(1)}, u32[]{:S(2)}, u32[]{:S(2)}) collective-permute-start(f32[5,1,128]{2,1,0:T(1,128)S(1)} %get-tuple-element.107), channel_id=1, source_target_pairs={{8,0},{16,8},{24,16},{9,1},{17,9},{25,17},{10,2},{18,10},{26,18},{... | collective-permute-start | bytes 7688 | tf_op jit(solution)/shard_map/ppermute | solution.py:33
  146.7 4.1 %collective-permute-start.4 = (f32[5,1,128]{2,1,0:T(1,128)S(1)}, f32[5,1,128]{2,1,0:T(1,128)S(1)}, u32[]{:S(2)}, u32[]{:S(2)}) collective-permute-start(f32[5,1,128]{2,1,0:T(1,128)S(1)} %get-tuple-element.102), channel_id=1, source_target_pairs={{0,8},{8,16},{16,24},{1,9},{9,17},{17,25},{2,10},{10,18},{18,26},{... | collective-permute-start | bytes 7688 | tf_op jit(solution)/shard_map/ppermute | solution.py:32
  149.5 5.5 %collective-permute-start.5 = (f32[5,1,128]{2,1,0:T(1,128)S(1)}, f32[5,1,128]{2,1,0:T(1,128)S(1)}, u32[]{:S(2)}, u32[]{:S(2)}) collective-permute-start(f32[5,1,128]{2,1,0:T(1,128)S(1)} %get-tuple-element.103), channel_id=1, source_target_pairs={{8,0},{16,8},{24,16},{9,1},{17,9},{25,17},{10,2},{18,10},{26,18},{... | collective-permute-start | bytes 7688 | tf_op jit(solution)/shard_map/ppermute | solution.py:33
  155.1 4.1 %collective-permute-start.6 = (f32[5,1,128]{2,1,0:T(1,128)S(1)}, f32[5,1,128]{2,1,0:T(1,128)S(1)}, u32[]{:S(2)}, u32[]{:S(2)}) collective-permute-start(f32[5,1,128]{2,1,0:T(1,128)S(1)} %get-tuple-element.98), channel_id=1, source_target_pairs={{0,8},{8,16},{16,24},{1,9},{9,17},{17,25},{2,10},{10,18},{18,26},{... | collective-permute-start | bytes 7688 | tf_op jit(solution)/shard_map/ppermute | solution.py:32
  157.9 5.5 %collective-permute-start.7 = (f32[5,1,128]{2,1,0:T(1,128)S(1)}, f32[5,1,128]{2,1,0:T(1,128)S(1)}, u32[]{:S(2)}, u32[]{:S(2)}) collective-permute-start(f32[5,1,128]{2,1,0:T(1,128)S(1)} %get-tuple-element.99), channel_id=1, source_target_pairs={{8,0},{16,8},{24,16},{9,1},{17,9},{25,17},{10,2},{18,10},{26,18},{... | collective-permute-start | bytes 7688 | tf_op jit(solution)/shard_map/ppermute | solution.py:33
  163.6 5.6 %collective-permute-start.8 = (f32[5,1,128]{2,1,0:T(1,128)S(1)}, f32[5,1,128]{2,1,0:T(1,128)S(1)}, u32[]{:S(2)}, u32[]{:S(2)}) collective-permute-start(f32[5,1,128]{2,1,0:T(1,128)S(1)} %get-tuple-element.94), channel_id=1, source_target_pairs={{0,8},{8,16},{16,24},{1,9},{9,17},{17,25},{2,10},{10,18},{18,26},{... | collective-permute-start | bytes 7688 | tf_op jit(solution)/shard_map/ppermute | solution.py:32
  166.4 5.5 %collective-permute-start.9 = (f32[5,1,128]{2,1,0:T(1,128)S(1)}, f32[5,1,128]{2,1,0:T(1,128)S(1)}, u32[]{:S(2)}, u32[]{:S(2)}) collective-permute-start(f32[5,1,128]{2,1,0:T(1,128)S(1)} %get-tuple-element.95), channel_id=1, source_target_pairs={{8,0},{16,8},{24,16},{9,1},{17,9},{25,17},{10,2},{18,10},{26,18},{... | collective-permute-start | bytes 7688 | tf_op jit(solution)/shard_map/ppermute | solution.py:33
where the time goes:
time: 234 us; the launch traced here: 232 us
  blocking collectives  74.7 us (32%)
  waiting for transfers between devices  57.6 us (25%)
  starting transfers between devices  32.2 us (14%)
  other arithmetic  22.3 us (10%)
  local copies, waits for them, and re-layouts  18.3 us (8%)
  between operations  17.1 us (7%)
  matrix products  9.95 us (4%)
    ppermute x6, waiting for transfers between devices, passed_along(): return lax.ppermute(block, axis, route)  42.4 us
    unnamed x1, blocking collectives  26.4 us
    psum x1, blocking collectives, body(): lax.psum(jnp.dot(weighted, half_field, precision=HIGH), 'vel')  21.3 us
    psum x1, blocking collectives, body(): lax.psum(jnp.dot(weighted, distribution, precision=HIGH), 'vel')  18.3 us
    ppermute x6, starting transfers between devices, passed_along(): return lax.ppermute(block, axis, route)  16.9 us
    ppermute x4, waiting for transfers between devices, extended(): after = lax.ppermute(first, axis, down)  15.2 us
    rev x2, local copies, waits for them, and re-layouts, body(): lax.associative_scan(affine_combine, (carry_rate[:, :half_nodes], drive_t...  9.93 us
    ppermute x4, starting transfers between devices, extended(): before = lax.ppermute(last, axis, up)  9.91 us
  transfers between devices with their start and end apart: 14, of which 10 were waited for; matrix products, arithmetic and copies ran while one was open for 0% of the time, Pallas kernels for 0%

commit v1 on v0

v1 whole, which is shorter than its diff:
```python
import functools
import math

import jax
import jax.numpy as jnp
import numpy as np
from jax import lax
from jax.experimental import pallas as pl
from jax.experimental.pallas import tpu as pltpu
from jax.sharding import PartitionSpec as P

NXI = 24
TUBES = 128
JACOBI = 4
NEWTON = 2
CHUNKS = 6
PROWS = 80
pseudo_rate = 1.0
MESH = pl.DeviceIdType.MESH


def hermite_rule(count):
    quarter = math.pi ** (-0.25)
    found = []
    last_slope = 1.0
    for index in range(count // 2):
        if index == 0:
            guess = math.sqrt(2.0 * count + 1.0) - 1.85575 * (2.0 * count + 1.0) ** (-0.16667)
        elif index == 1:
            guess = guess - 1.14 * count**0.426 / guess
        elif index == 2:
            guess = 1.86 * guess - 0.86 * found[0][0]
        elif index == 3:
            guess = 1.91 * guess - 0.91 * found[1][0]
        else:
            guess = 2.0 * guess - found[index - 2][0]
        for repeat in range(60):
            current = quarter
            previous = 0.0
            for order in range(count):
                older = previous
                previous = current
                current = (
                    guess * math.sqrt(2.0 / (order + 1)) * previous
                    - math.sqrt(order / (order + 1.0)) * older
                )
            last_slope = math.sqrt(2.0 * count) * previous
            guess = guess - current / last_slope
        found.append((guess, 2.0 / (last_slope * last_slope)))
    positive = found[::-1]
    points = [-pair[0] for pair in found] + [pair[0] for pair in positive]
    weights = [pair[1] for pair in found] + [pair[1] for pair in positive]
    return (np.array(points), np.array(weights))


def tables():
    points, weights = hermite_rule(NXI)
    h = weights / math.sqrt(math.pi)
    y = np.repeat(points, NXI)
    z = np.tile(points, NXI)
    g = np.repeat(h, NXI) * np.tile(h, NXI)
    e = y * y + z * z - 1.0
    rows = np.concatenate([g, g * y, g * z, g * e, y, z, e]).astype(np.float32)
    cols = np.zeros((40, 128))
    x = points
    listed = [np.abs(x), 2.0 * x, (x * x - 0.5) / 1.5, h, h * x, h * (x * x - 0.5), x]
    for k, column in enumerate(listed):
        cols[:24, k] = column
    for lane in range(3):
        cols[24:32, lane] = x[lane * 8 : lane * 8 + 8]
        cols[32:40, lane] = h[lane * 8 : lane * 8 + 8]
    return rows, cols.astype(np.float32)


def kernel(
    n_sec, n_vel, length, rows,
    table, cols, dist, coll, lower, upper, diag,
    syn_out, grow_out, macro_out,
    dv, syn, out_p, out_n, in_p, in_n, s_part, s_recv, s_all, pb,
    om, hm, co, mac, t_all, w_tab, t_loc, ld_own, ld_sec, ld_rv, ld_rs,
    dist_sem, syn_sem, p_send, p_recv, n_send, n_recv,
    a1_send, a1_recv, a2_send, a2_recv, a3_send, a3_recv,
    pb_send, pb_recv, b1_send, b1_recv, b2_send, b2_recv,
):
    s = lax.axis_index("sec")
    v = lax.axis_index("vel")
    total = n_sec * length
    slices = 4 * length
    pairs = rows // 2
    per = pairs // CHUNKS
    all_rows = NXI * NXI

    load = pltpu.make_async_copy(dist, dv, dist_sem)
    load.start()
    barrier = pltpu.get_barrier_semaphore()
    for d in range(1, n_vel):
        pl.semaphore_signal(
            barrier, inc=1, device_id={"vel": lax.rem(v + d, n_vel)}, device_id_type=MESH
        )
    for d in range(1, n_sec):
        pl.semaphore_signal(
            barrier, inc=1, device_id={"sec": lax.rem(s + d, n_sec)}, device_id_type=MESH
        )

    def remote(src, dst, send, recv, where):
        return pltpu.make_async_remote_copy(
            src_ref=src, dst_ref=dst, send_sem=send, recv_sem=recv,
            device_id=where, device_id_type=MESH,
        )

    def column(k):
        return jnp.broadcast_to(cols[0:24, k : k + 1], (24, TUBES))

    sub = lax.broadcasted_iota(jnp.int32, (8, TUBES), 0)
    low = sub < 4
    pos = lax.broadcasted_iota(jnp.int32, (24, TUBES), 0) >= 12
    reach = column(0) * float(total)

    for p in range(length):
        lanes = slice(p * TUBES, (p + 1) * TUBES)
        base = (s * length + p) * PROWS
        for k, block in enumerate((lower, upper, diag)):
            for e in range(25):
                pb[pl.ds(base + k * 25 + e, 1), :] = block[e : e + 1, lanes]
        pb[pl.ds(base + 75, 1), :] = coll[0:1, lanes]
    inv, rate = [], []
    for p in range(length):
        den = reach + coll[0:1, p * TUBES : (p + 1) * TUBES] + pseudo_rate
        i = 1.0 / den
        inv.append(i)
        rate.append(reach * i)
    zero = jnp.zeros((24, TUBES), jnp.float32)
    w = [[zero] * length for _ in range(length)]
    a = [zero] * length
    fw = None
    for p in range(length):
        row = [rate[p] * e for e in fw[0]] + [inv[p]] if fw else [inv[p]]
        carry = rate[p] * fw[1] if fw else rate[p]
        fw = (row, carry)
        for q in range(p + 1):
            w[p][q] = jnp.where(pos, row[q], w[p][q])
        a[p] = jnp.where(pos, carry, a[p])
    bw = None
    for p in reversed(range(length)):
        row = [inv[p]] + [rate[p] * e for e in bw[0]] if bw else [inv[p]]
        carry = rate[p] * bw[1] if bw else rate[p]
        bw = (row, carry)
        for k in range(len(row)):
            w[p][p + k] = jnp.where(pos, w[p][p + k], row[k])
        a[p] = jnp.where(pos, a[p], carry)
    for p in range(length):
        for q in range(length):
            w_tab[p * (length + 1) + q] = w[p][q]
        w_tab[p * (length + 1) + length] = a[p]
    last = [jnp.where(pos, w[length - 1][q], w[0][q]) for q in range(length)]
    through = jnp.where(pos, a[length - 1], a[0])
    mix = through[8:16]
    mix_r = pltpu.roll(mix, 4, 0)
    thr_n = jnp.concatenate([through[0:8], through[0:8], jnp.where(low, mix, mix_r)], axis=0)
    thr_p = jnp.concatenate([through[16:24], through[16:24], jnp.where(low, mix_r, mix)], axis=0)

    @pl.when(s == 0)
    def _():
        in_p[...] = jnp.zeros_like(in_p)

    @pl.when(s == n_sec - 1)
    def _():
        in_n[...] = jnp.zeros_like(in_n)

    pl.semaphore_wait(barrier, n_vel + n_sec - 2)
    load.wait()

    def chunk(c):
        return pl.ds(c * per, per)

    def pos_copy(c):
        to = jnp.minimum(s + 1, n_sec - 1)
        return remote(out_p.at[chunk(c)], in_p.at[chunk(c)], p_send.at[c], p_recv.at[c], {"sec": to})

    def neg_copy(c):
        to = jnp.maximum(s - 1, 0)
        return remote(out_n.at[chunk(c)], in_n.at[chunk(c)], n_send.at[c], n_recv.at[c], {"sec": to})

    def first_pass(k, acc):
        acc = list(acc)
        bs = []
        for half in range(2):
            r = 2 * k + half
            at = v * rows + r
            d = [
                dv[pl.ds(pl.multiple_of(k * 48, 8) + half * 24, 24), p * TUBES : (p + 1) * TUBES]
                for p in range(length)
            ]
            for q in range(4):
                scale = table[q * all_rows + at]
                for p in range(length):
                    acc[p * 4 + q] = acc[p * 4 + q] + scale * d[p]
            b = last[0] * d[0]
            for p in range(1, length):
                b = b + last[p] * d[p]
            bs.append(b)
        b0, b1 = bs
        out_n[k, 0:8] = b0[0:8]
        out_n[k, 8:16] = b1[0:8]
        out_n[k, 16:24] = jnp.where(low, b0[8:16], pltpu.roll(b1[8:16], 4, 0))
        out_p[k, 0:8] = b0[16:24]
        out_p[k, 8:16] = b1[16:24]
        out_p[k, 16:24] = jnp.where(low, pltpu.roll(b0[8:16], 4, 0), b1[8:16])
        return tuple(acc)

    acc = (zero,) * slices
    for c in range(CHUNKS):
        acc = lax.fori_loop(c * per, (c + 1) * per, first_pass, acc)

        @pl.when(s == 0)
        def _():
            pos_copy(c).start()

        @pl.when(s == n_sec - 1)
        def _():
            neg_copy(c).start()

    for k in range(slices):
        s_part[k] = acc[k]

    def when_owner(index, run):
        if n_vel == slices:
            run()
        else:
            pl.when(index < slices)(run)

    def a1(d):
        to = lax.rem(v + d, n_vel)
        slot = jnp.minimum(to, slices - 1)
        return remote(s_part.at[slot], s_recv.at[d - 1], a1_send.at[d - 1], a1_recv.at[d - 1], {"vel": to})

    for d in range(1, n_vel):
        when_owner(lax.rem(v + d, n_vel), lambda: a1(d).start())

    own = pl.ds(s * length * PROWS, length * PROWS)

    def pb_copy(d):
        to = lax.rem(s + d, n_sec)
        return remote(pb.at[own], pb.at[own], pb_send.at[d - 1], pb_recv.at[d - 1], {"sec": to})

    def pb_wait(d):
        frm = lax.rem(s + n_sec - d, n_sec)
        there = pl.ds(frm * length * PROWS, length * PROWS)
        remote(pb.at[there], pb.at[there], pb_send.at[d - 1], pb_recv.at[d - 1], {"sec": frm}).wait_recv()

    for d in range(1, n_sec):
        pb_copy(d).start()

    mine = jnp.minimum(v, slices - 1)

    def a2(d, slot, to):
        return remote(
            s_all.at[mine, slot], s_all.at[mine, slot], a2_send.at[d - 1], a2_recv.at[d - 1], {"sec": to}
        )

    def reduce_slices():
        got = s_part[mine]
        for d in range(1, n_vel):
            a1(d).wait_recv()
            got = got + s_recv[d - 1]
        s_all[mine, s] = got
        for d in range(1, n_sec):
            a2(d, s, lax.rem(s + d, n_sec)).start()

    when_owner(v, reduce_slices)

    def relay(c):
        def forward_pos():
            pos_copy(c).wait_recv()

            @pl.when(s < n_sec - 1)
            def _():
                out_p[chunk(c)] = out_p[chunk(c)] + thr_p[None] * in_p[chunk(c)]
                pos_copy(c).start()

        def forward_neg():
            neg_copy(c).wait_recv()

            @pl.when(s > 0)
            def _():
                out_n[chunk(c)] = out_n[chunk(c)] + thr_n[None] * in_n[chunk(c)]
                neg_copy(c).start()

        @pl.when(s < n_sec // 2)
        def _():
            pl.when(s > 0)(forward_pos)
            forward_neg()

        @pl.when(s >= n_sec // 2)
        def _():
            pl.when(s < n_sec - 1)(forward_neg)
            forward_pos()

    def a3(d, slot, to):
        return remote(s_all.at[slot], s_all.at[slot], a3_send.at[d - 1], a3_recv.at[d - 1], {"vel": to})

    def gather_slices():
        for d in range(1, n_sec):
            frm = lax.rem(s + n_sec - d, n_sec)
            a2(d, frm, frm).wait_recv()
        for d in range(1, n_vel):
            a3(d, mine, lax.rem(v + d, n_vel)).start()

    relay(0)
    when_owner(v, gather_slices)
    for c in range(1, CHUNKS):
        relay(c)
    for d in range(1, n_vel):
        frm = lax.rem(v + n_vel - d, n_vel)
        when_owner(frm, lambda: a3(d, jnp.minimum(frm, slices - 1), frm).wait_recv())
    for d in range(1, n_sec):
        pb_wait(d)

    hx, hxx, hxe = column(3), column(4), column(5)
    x2, en = column(1), column(2)

    def total_of(value):
        return jnp.sum(value, axis=0, keepdims=True)

    for at in range(total):
        sec, p = at // length, at % length
        s0, s2, s3, s4 = [s_all[p * 4 + q, sec] for q in range(4)]
        om[0 * total + at : 0 * total + at + 1] = total_of(hx * s0)
        om[1 * total + at : 1 * total + at + 1] = total_of(hxx * s0)
        om[2 * total + at : 2 * total + at + 1] = total_of(hx * s2)
        om[3 * total + at : 3 * total + at + 1] = total_of(hx * s3)
        om[4 * total + at : 4 * total + at + 1] = total_of(hxe * s0 + hx * s4)

    thick, invs, rates = [], [], []
    for at in range(total):
        t = pb[at * PROWS + 75 : at * PROWS + 76]
        i = 1.0 / (reach + t + pseudo_rate)
        thick.append(t)
        invs.append(i)
        rates.append(reach * i)
    turned = [jnp.where(pos, rates[i], rates[total - 1 - i]) for i in range(total)]

    def sweep(drive):
        found, carried = [], None
        for i in range(total):
            here = jnp.where(pos, drive[i], drive[total - 1 - i])
            carried = here if carried is None else turned[i] * carried + here
            found.append(carried)
        return [jnp.where(pos, found[i], found[total - 1 - i]) for i in range(total)]

    halves = {}
    for q, norm in enumerate((1.0, 0.5, 0.5, 1.0)):
        goals, parts = [], []
        for at in range(total):
            m = [om[j * total + at : j * total + at + 1] for j in range(5)]
            if q == 0:
                goal = thick[at] * (m[0] + x2 * m[1] + en * m[4])
            elif q == 3:
                goal = jnp.broadcast_to(thick[at] * m[4] * (1.0 / 1.5), (24, TUBES))
            else:
                goal = jnp.broadcast_to(thick[at] * m[q + 1] * 2.0, (24, TUBES))
            sec, p = at // length, at % length
            goals.append(goal * invs[at])
            parts.append((s_all[p * 4 + q, sec] + norm * goal) * invs[at])
        swept = sweep(goals)
        for at in range(total):
            t_all[q * total + at] = swept[at]
        swept = sweep(parts)
        for at in range(total):
            f = swept[at]
            if q == 0:
                hm[at : at + 1] = total_of(hx * f)
                hm[total + at : total + at + 1] = total_of(hxx * f)
                halves[at] = hxe * f
            elif q == 3:
                hm[4 * total + at : 4 * total + at + 1] = total_of(halves[at] + hx * f)
            else:
                j = q + 1
                hm[j * total + at : j * total + at + 1] = total_of(hx * f)

    place = lax.broadcasted_iota(jnp.int32, (total, TUBES), 0)
    old = [om[j * total : (j + 1) * total] for j in range(5)]
    half = [hm[j * total : (j + 1) * total] for j in range(5)]
    resid = [half[j] - old[j] for j in range(5)]

    def entry(e):
        return pb[pl.ds(e, total, stride=PROWS), :]

    def apply_block(first, vector):
        out = []
        for i in range(5):
            value = entry(first + i * 5) * vector[0]
            for j in range(1, 5):
                value = value + entry(first + i * 5 + j) * vector[j]
            out.append(value)
        return out

    corr = apply_block(50, resid)
    for _ in range(JACOBI):
        left = [jnp.where(place == 0, 0.0, pltpu.roll(c, 1, 0)) for c in corr]
        right = [jnp.where(place == total - 1, 0.0, pltpu.roll(c, total - 1, 0)) for c in corr]
        lo = apply_block(0, left)
        up = apply_block(25, right)
        corr = apply_block(50, [resid[j] - lo[j] - up[j] for j in range(5)])
    goal = []
    for j in range(5):
        macro = half[j] + corr[j]
        co[j * total : (j + 1) * total] = corr[j]
        mac[j * total : (j + 1) * total] = macro
        if j < 2:
            change = jnp.sum(old[j] - macro, axis=0, keepdims=True)
            goal.append(jnp.sum(change, axis=1, keepdims=True))
    for p in range(length):
        at = s * length + p
        c = [co[pl.ds(j * total + at, 1), :] for j in range(5)]
        for j in range(5):
            macro_out[j : j + 1, p * TUBES : (p + 1) * TUBES] = mac[pl.ds(j * total + at, 1), :]
        t_loc[p * 4 + 0] = t_all[0 * total + at] + (c[0] + x2 * c[1] + en * c[4])
        t_loc[p * 4 + 1] = t_all[1 * total + at] + 2.0 * c[2]
        t_loc[p * 4 + 2] = t_all[2 * total + at] + 2.0 * c[3]
        t_loc[p * 4 + 3] = t_all[3 * total + at] + c[4] * (1.0 / 1.5)

    def second_pass(k, acc):
        n_mix, p_mix = in_n[k, 16:24], in_p[k, 16:24]
        flow = (
            jnp.concatenate(
                [in_n[k, 0:8], jnp.where(low, n_mix, pltpu.roll(p_mix, 4, 0)), in_p[k, 0:8]], axis=0
            ),
            jnp.concatenate(
                [in_n[k, 8:16], jnp.where(low, pltpu.roll(n_mix, 4, 0), p_mix), in_p[k, 8:16]], axis=0
            ),
        )
        for half_row in range(2):
            at = v * rows + 2 * k + half_row
            here = pl.ds(pl.multiple_of(k * 48, 8) + half_row * 24, 24)
            g = table[at]
            y = table[4 * all_rows + at]
            z = table[5 * all_rows + at]
            e = table[6 * all_rows + at]
            d = [dv[here, p * TUBES : (p + 1) * TUBES] for p in range(length)]
            size = None
            for p in range(length):
                f = t_loc[p * 4] + y * t_loc[p * 4 + 1] + z * t_loc[p * 4 + 2] + e * t_loc[p * 4 + 3]
                f = f + w_tab[p * (length + 1) + length] * flow[half_row]
                for q in range(length):
                    f = f + w_tab[p * (length + 1) + q] * d[q]
                syn[here, p * TUBES : (p + 1) * TUBES] = f
                size = jnp.abs(f) if size is None else size + jnp.abs(f)
            acc = acc + g * size
        return acc

    acc = zero
    stores = []
    for c in range(CHUNKS):
        acc = lax.fori_loop(c * per, (c + 1) * per, second_pass, acc)
        part = pl.ds(c * per * 48, per * 48)
        store = pltpu.make_async_copy(syn.at[part], syn_out.at[part], syn_sem.at[c])
        store.start()
        stores.append(store)

    lane = lax.broadcasted_iota(jnp.int32, (8, TUBES), 1)
    one = jnp.sum(acc, axis=1, keepdims=True)
    packed = jnp.where(lane == 0, one[0:8], jnp.where(lane == 1, one[8:16], one[16:24]))
    ld_own[...] = packed
    b1 = [
        remote(ld_own, ld_rv.at[d - 1], b1_send.at[d - 1], b1_recv.at[d - 1],
               {"vel": lax.rem(v + d, n_vel)})
        for d in range(1, n_vel)
    ]
    for copy in b1:
        copy.start()
    for d in range(1, n_vel):
        b1[d - 1].wait_recv()
        packed = packed + ld_rv[d - 1]
    ld_sec[...] = packed
    b2 = [
        remote(ld_sec, ld_rs.at[d - 1], b2_send.at[d - 1], b2_recv.at[d - 1],
               {"sec": lax.rem(s + d, n_sec)})
        for d in range(1, n_sec)
    ]
    for copy in b2:
        copy.start()
    for d in range(1, n_sec):
        b2[d - 1].wait_recv()
        packed = packed + ld_rs[d - 1]

    signed = cols[24:32, :]
    loaded = cols[32:40, :] * packed

    def everything(value):
        return jnp.sum(jnp.sum(value, axis=0, keepdims=True), axis=1, keepdims=True)

    shift_mass = jnp.zeros((1, 1), jnp.float32)
    shift_flow = jnp.zeros((1, 1), jnp.float32)
    for turn in range(NEWTON):
        if turn == 0:
            scaled = loaded
            miss_mass, miss_flow = -goal[0], -goal[1]
        else:
            growth = jnp.exp(shift_mass + shift_flow * signed)
            scaled = loaded * growth
            excess = loaded * (growth - 1.0)
            miss_mass = everything(excess) - goal[0]
            miss_flow = everything(excess * signed) - goal[1]
        m0 = everything(scaled)
        m1 = everything(scaled * signed)
        m2 = everything(scaled * signed * signed)
        determinant = m0 * m2 - m1 * m1
        new_mass = shift_mass - (m2 * miss_mass - m1 * miss_flow) / determinant
        shift_flow = shift_flow - (m0 * miss_flow - m1 * miss_mass) / determinant
        shift_mass = new_mass
    grow_out[...] = jnp.exp(shift_mass + shift_flow * column(6)) - 1.0

    for c in range(CHUNKS):
        stores[c].wait()

        @pl.when(s < n_sec - 1)
        def _():
            pos_copy(c).wait_send()

        @pl.when(s > 0)
        def _():
            neg_copy(c).wait_send()

    for d in range(1, n_vel):
        when_owner(lax.rem(v + d, n_vel), lambda: a1(d).wait_send())
        when_owner(v, lambda: a3(d, mine, lax.rem(v + d, n_vel)).wait_send())
        b1[d - 1].wait_send()
    for d in range(1, n_sec):
        pb_copy(d).wait_send()
        when_owner(v, lambda: a2(d, s, lax.rem(s + d, n_sec)).wait_send())
        b2[d - 1].wait_send()


def body(n_sec, n_vel, distribution, collision, lower_blocks, upper_blocks, diag_inverse):
    nodes, cells = distribution.shape
    length = cells // TUBES
    rows = nodes // NXI
    pairs = rows // 2
    slices = 4 * length
    total = n_sec * length
    row_table, col_table = tables()
    f32 = jnp.float32
    vmem = pl.BlockSpec(memory_space=pltpu.VMEM)
    dma = pltpu.SemaphoreType.DMA
    syn, grow, macro = pl.pallas_call(
        functools.partial(kernel, n_sec, n_vel, length, rows),
        out_shape=(
            jax.ShapeDtypeStruct((nodes, cells), f32),
            jax.ShapeDtypeStruct((NXI, TUBES), f32),
            jax.ShapeDtypeStruct((5, cells), f32),
        ),
        in_specs=[
            pl.BlockSpec(memory_space=pltpu.SMEM), vmem, pl.BlockSpec(memory_space=pl.ANY),
            vmem, vmem, vmem, vmem,
        ],
        out_specs=(pl.BlockSpec(memory_space=pl.ANY), vmem, vmem),
        scratch_shapes=[
            pltpu.VMEM((nodes, cells), f32),
            pltpu.VMEM((nodes, cells), f32),
            pltpu.VMEM((pairs, 24, TUBES), f32),
            pltpu.VMEM((pairs, 24, TUBES), f32),
            pltpu.VMEM((pairs, 24, TUBES), f32),
            pltpu.VMEM((pairs, 24, TUBES), f32),
            pltpu.VMEM((slices, NXI, TUBES), f32),
            pltpu.VMEM((n_vel - 1, NXI, TUBES), f32),
            pltpu.VMEM((slices, n_sec, NXI, TUBES), f32),
            pltpu.VMEM((total * PROWS, TUBES), f32),
            pltpu.VMEM((5 * total, TUBES), f32),
            pltpu.VMEM((5 * total, TUBES), f32),
            pltpu.VMEM((5 * total, TUBES), f32),
            pltpu.VMEM((5 * total, TUBES), f32),
            pltpu.VMEM((4 * total, NXI, TUBES), f32),
            pltpu.VMEM((length * (length + 1), NXI, TUBES), f32),
            pltpu.VMEM((slices, NXI, TUBES), f32),
            pltpu.VMEM((8, TUBES), f32),
            pltpu.VMEM((8, TUBES), f32),
            pltpu.VMEM((n_vel - 1, 8, TUBES), f32),
            pltpu.VMEM((n_sec - 1, 8, TUBES), f32),
            dma,
            dma((CHUNKS,)), dma((CHUNKS,)), dma((CHUNKS,)), dma((CHUNKS,)), dma((CHUNKS,)),
            dma((n_vel - 1,)), dma((n_vel - 1,)),
            dma((n_sec - 1,)), dma((n_sec - 1,)),
            dma((n_vel - 1,)), dma((n_vel - 1,)),
            dma((n_sec - 1,)), dma((n_sec - 1,)),
            dma((n_vel - 1,)), dma((n_vel - 1,)),
            dma((n_sec - 1,)), dma((n_sec - 1,)),
        ],
        compiler_params=pltpu.CompilerParams(
            collective_id=0, has_side_effects=True, vmem_limit_bytes=40 * 1024 * 1024
        ),
    )(
        jnp.asarray(row_table), jnp.asarray(col_table), distribution,
        collision.reshape(1, cells), lower_blocks, upper_blocks, diag_inverse,
    )
    field = syn.reshape(rows, NXI, cells)
    new = field + jnp.abs(field) * grow[None, :, 0:1]
    return (new.reshape(nodes, cells), macro)


def solution(mesh):
    in_specs = (P("vel", "sec"), P("sec"), P(None, "sec"), P(None, "sec"), P(None, "sec"))
    out_specs = (P("vel", "sec"), P(None, "sec"))
    run = functools.partial(body, mesh.shape["sec"], mesh.shape["vel"])
    return jax.shard_map(run, mesh=mesh, in_specs=in_specs, out_specs=out_specs, check_vma=False)
```

time: 234 us -> 69 us (0.29)
  blocking collectives: 74.7 us -> 0 us
  Pallas kernels: 0 us -> 59.7 us
  waiting for transfers between devices: 57.6 us -> 0 us
  starting transfers between devices: 32.2 us -> 0 us
  other arithmetic: 22.3 us -> 1.5 us
  between operations: 17.1 us -> 0.66 us
  local copies, waits for them, and re-layouts: 18.3 us -> 6.67 us
  matrix products: 9.95 us -> 0 us
    pallas_call x0 -> x1, Pallas kernels: none -> 59.7 us  [body(): pl.pallas_call(functools.partial(kernel, n_sec, n_vel, length, rows), out...]
    ppermute x14 -> x0, waiting for transfers between devices: 57.6 us -> none  [the longest x6 42.4 us: passed_along(): return lax.ppermute(block, axis, route)]
    psum x3 -> x0, blocking collectives: 48.3 us -> none  [the longest x1 21.3 us: body(): lax.psum(jnp.dot(weighted, half_field, precision=HIGH), 'vel')]
    ppermute x14 -> x0, starting transfers between devices: 32.2 us -> none  [the longest x6 16.9 us: passed_along(): return lax.ppermute(block, axis, route)]
    unnamed x1 -> x0, blocking collectives: 26.4 us -> none
    add x13 -> x1, other arithmetic: 11.9 us -> 1.5 us  [body(): new = field + jnp.abs(field) * grow[None, :, 0:1]]
    dot_general x4 -> x0, matrix products: 9.95 us -> none  [the longest x1 3.8 us: body(): target = jnp.dot(rebuild.T, old_moments, precision=HIGH)]
    rev x2 -> x0, local copies, waits for them, and re-layouts: 9.93 us -> none  [body(): lax.associative_scan(affine_combine, (carry_rate[:, :half_nodes], drive_t...]
  transfers between devices with their start and end apart: 14 -> 0, of which waited for: 10 -> 0; matrix products, arithmetic and copies ran while one was open for 0% -> 0% of each run, Pallas kernels for 0% -> 0%
where the time goes in v1:
time: 69 us; the launch traced here: 68.5 us
  Pallas kernels  59.7 us (87%)
  local copies, waits for them, and re-layouts  6.67 us (10%)
  other arithmetic  1.5 us (2%)
    pallas_call x1, Pallas kernels, body(): pl.pallas_call(functools.partial(kernel, n_sec, n_vel, length, rows), out...  59.7 us
    unnamed x15, local copies, waits for them, and re-layouts  6.46 us
    add x1, other arithmetic, body(): new = field + jnp.abs(field) * grow[None, :, 0:1]  1.5 us

profile of v1, /device:TPU:0, one launch (start us, length us, event | category | flops | bytes accessed | tf_op | source)
XLA Modules:
  0.0 68.5 jit_solution(2111701912471725943)
XLA Ops:
  0.6 0.0 copy-start
  0.6 1.5 %copy-done = f32[1728,256]{1,0:T(8,128)S(1)} copy-done((f32[1728,256]{1,0:T(8,128)S(1)}, f32[1728,256]{1,0:T(8,128)}, u32[]{:S(2)}) %copy-start) | copy-done | bytes 1769496
  2.1 0.0 copy-start.1
  2.1 0.8 %copy-done.1 = f32[25,256]{1,0:T(8,128)S(1)} copy-done((f32[25,256]{1,0:T(8,128)S(1)}, f32[25,256]{1,0:T(8,128)}, u32[]{:S(2)}) %copy-start.1) | copy-done | bytes 25624
  2.9 0.0 copy-start.2
  2.9 0.8 %copy-done.2 = f32[25,256]{1,0:T(8,128)S(1)} copy-done((f32[25,256]{1,0:T(8,128)S(1)}, f32[25,256]{1,0:T(8,128)}, u32[]{:S(2)}) %copy-start.2) | copy-done | bytes 25624
  3.6 0.0 copy-start.3
  3.6 0.8 %copy-done.3 = f32[25,256]{1,0:T(8,128)S(1)} copy-done((f32[25,256]{1,0:T(8,128)S(1)}, f32[25,256]{1,0:T(8,128)}, u32[]{:S(2)}) %copy-start.3) | copy-done | bytes 25624
  4.4 0.0 copy-start.4
  4.4 0.7 %copy-done.4 = f32[40,128]{1,0:T(8,128)S(1)} copy-done((f32[40,128]{1,0:T(8,128)S(1)}, f32[40,128]{1,0:T(8,128)}, u32[]{:S(2)}) %copy-start.4) | copy-done | bytes 20504
  5.1 0.0 copy-start.5
  5.1 0.7 %copy-done.5 = f32[4032]{0:T(1024)S(1)} copy-done((f32[4032]{0:T(1024)S(1)}, f32[4032]{0:T(1024)}, u32[]{:S(2)}) %copy-start.5) | copy-done | bytes 16152
  5.8 0.0 copy-start.6
  5.8 0.7 copy-done.6
  6.5 59.7 %shard_map.86 = (f32[1728,256]{1,0:T(8,128)S(1)}, f32[24,128]{1,0:T(8,128)S(1)}, f32[5,256]{1,0:T(8,128)S(1)}) custom-call(f32[4032]{0:T(1024)S(1)} %copy-done.5, f32[40,128]{1,0:T(8,128)S(1)} %copy-done.4, f32[1728,256]{1,0:T(8,128)S(1)} %copy-done, f32[1,256]{1,0:T(1,128)S(1)} %bitcast.1, f32[25,256]{1,0:T(8,128)S(1)} %copy-done.1, ...), custom_call_target="tpu_custom_call" | custom-call | tf_op jit(solution)/shard_map/pallas_call | solution.py:546
  66.2 0.1 slice_reduce_fusion
  66.3 0.1 mul.17
  66.4 1.5 %multiply_add_fusion = f32[1728,256]{1,0:T(8,128)} fusion(f32[1728,256]{1,0:T(8,128)S(1)} %get-tuple-element.5, f32[1728]{0:T(1024)S(1)} %mul.17), kind=kLoop, calls=%fused_computation | loop fusion | flops 1327104 | bytes 3545856 | tf_op jit(solution)/shard_map/add | solution.py:597
  67.9 0.6 copy.10
  (1 shorter events, 0.0 us)
Async XLA Ops:
  0.6 1.5 %copy-start = (f32[1728,256]{1,0:T(8,128)S(1)}, f32[1728,256]{1,0:T(8,128)}, u32[]{:S(2)}) copy-start(f32[1728,256]{1,0:T(8,128)} %dist.1) | copy-start | bytes 5308420
  2.1 0.8 %copy-start.1 = (f32[25,256]{1,0:T(8,128)S(1)}, f32[25,256]{1,0:T(8,128)}, u32[]{:S(2)}) copy-start(f32[25,256]{1,0:T(8,128)} %lower.1) | copy-start | bytes 76804
  2.9 0.8 %copy-start.2 = (f32[25,256]{1,0:T(8,128)S(1)}, f32[25,256]{1,0:T(8,128)}, u32[]{:S(2)}) copy-start(f32[25,256]{1,0:T(8,128)} %upper.1) | copy-start | bytes 76804
  3.6 0.8 %copy-start.3 = (f32[25,256]{1,0:T(8,128)S(1)}, f32[25,256]{1,0:T(8,128)}, u32[]{:S(2)}) copy-start(f32[25,256]{1,0:T(8,128)} %diag.1) | copy-start | bytes 76804
  4.4 0.7 %copy-start.4 = (f32[40,128]{1,0:T(8,128)S(1)}, f32[40,128]{1,0:T(8,128)}, u32[]{:S(2)}) copy-start(f32[40,128]{1,0:T(8,128)} %constant.5.clone.cols) | copy-start | bytes 61444
  5.1 0.7 %copy-start.5 = (f32[4032]{0:T(1024)S(1)}, f32[4032]{0:T(1024)}, u32[]{:S(2)}) copy-start(f32[4032]{0:T(1024)} %constant.4.clone.table) | copy-start | bytes 48388
  5.8 0.7 copy-start.6

commit v2 on v1

--- a/solution.py
+++ b/solution.py
@@ -74,8 +74,9 @@
 
 def kernel(
     n_sec, n_vel, length, rows,
-    table, cols, dist, coll, lower, upper, diag,
+    table_in, cols_in, dist, coll_in, lower_in, upper_in, diag_in,
     syn_out, grow_out, macro_out,
+    table, cols, coll, lower, upper, diag, small_sem,
     dv, syn, out_p, out_n, in_p, in_n, s_part, s_recv, s_all, pb,
     om, hm, co, mac, t_all, w_tab, t_loc, ld_own, ld_sec, ld_rv, ld_rs,
     dist_sem, syn_sem, p_send, p_recv, n_send, n_recv,
@@ -91,7 +92,20 @@
     all_rows = NXI * NXI
 
     load = pltpu.make_async_copy(dist, dv, dist_sem)
+    small = [
+        pltpu.make_async_copy(src, dst, small_sem.at[k])
+        for k, (src, dst) in enumerate(
+            (
+                (cols_in, cols), (coll_in, coll), (table_in, table),
+                (lower_in, lower), (upper_in, upper), (diag_in, diag),
+            )
+        )
+    ]
+    for copy in small[:3]:
+        copy.start()
     load.start()
+    for copy in small[3:]:
+        copy.start()
     barrier = pltpu.get_barrier_semaphore()
     for d in range(1, n_vel):
         pl.semaphore_signal(
@@ -111,18 +125,13 @@
     def column(k):
         return jnp.broadcast_to(cols[0:24, k : k + 1], (24, TUBES))
 
+    small[0].wait()
+    small[1].wait()
     sub = lax.broadcasted_iota(jnp.int32, (8, TUBES), 0)
     low = sub < 4
     pos = lax.broadcasted_iota(jnp.int32, (24, TUBES), 0) >= 12
     reach = column(0) * float(total)
 
-    for p in range(length):
-        lanes = slice(p * TUBES, (p + 1) * TUBES)
-        base = (s * length + p) * PROWS
-        for k, block in enumerate((lower, upper, diag)):
-            for e in range(25):
-                pb[pl.ds(base + k * 25 + e, 1), :] = block[e : e + 1, lanes]
-        pb[pl.ds(base + 75, 1), :] = coll[0:1, lanes]
     inv, rate = [], []
     for p in range(length):
         den = reach + coll[0:1, p * TUBES : (p + 1) * TUBES] + pseudo_rate
@@ -168,6 +177,7 @@
         in_n[...] = jnp.zeros_like(in_n)
 
     pl.semaphore_wait(barrier, n_vel + n_sec - 2)
+    small[2].wait()
     load.wait()
 
     def chunk(c):
@@ -237,6 +247,15 @@
     for d in range(1, n_vel):
         when_owner(lax.rem(v + d, n_vel), lambda: a1(d).start())
 
+    for copy in small[3:]:
+        copy.wait()
+    for p in range(length):
+        lanes = slice(p * TUBES, (p + 1) * TUBES)
+        base = (s * length + p) * PROWS
+        for k, block in enumerate((lower, upper, diag)):
+            for e in range(25):
+                pb[pl.ds(base + k * 25 + e, 1), :] = block[e : e + 1, lanes]
+        pb[pl.ds(base + 75, 1), :] = coll[0:1, lanes]
     own = pl.ds(s * length * PROWS, length * PROWS)
 
     def pb_copy(d):
@@ -306,10 +325,14 @@
         for d in range(1, n_vel):
             a3(d, mine, lax.rem(v + d, n_vel)).start()
 
-    relay(0)
     when_owner(v, gather_slices)
-    for c in range(1, CHUNKS):
-        relay(c)
+    inner = jnp.logical_and(s > 0, s < n_sec - 1)
+
+    @pl.when(inner)
+    def _():
+        for c in range(CHUNKS):
+            relay(c)
+
     for d in range(1, n_vel):
         frm = lax.rem(v + n_vel - d, n_vel)
         when_owner(frm, lambda: a3(d, jnp.minimum(frm, slices - 1), frm).wait_recv())
@@ -383,15 +406,14 @@
     half = [hm[j * total : (j + 1) * total] for j in range(5)]
     resid = [half[j] - old[j] for j in range(5)]
 
-    def entry(e):
-        return pb[pl.ds(e, total, stride=PROWS), :]
+    entries = [pb[pl.ds(e, total, stride=PROWS), :] for e in range(75)]
 
     def apply_block(first, vector):
         out = []
         for i in range(5):
-            value = entry(first + i * 5) * vector[0]
+            value = entries[first + i * 5] * vector[0]
             for j in range(1, 5):
-                value = value + entry(first + i * 5 + j) * vector[j]
+                value = value + entries[first + i * 5 + j] * vector[j]
             out.append(value)
         return out
 
@@ -419,6 +441,11 @@
         t_loc[p * 4 + 1] = t_all[1 * total + at] + 2.0 * c[2]
         t_loc[p * 4 + 2] = t_all[2 * total + at] + 2.0 * c[3]
         t_loc[p * 4 + 3] = t_all[3 * total + at] + c[4] * (1.0 / 1.5)
+
+    @pl.when(jnp.logical_not(inner))
+    def _():
+        for c in range(CHUNKS):
+            relay(c)
 
     def second_pass(k, acc):
         n_mix, p_mix = in_n[k, 16:24], in_p[k, 16:24]
@@ -550,12 +577,16 @@
             jax.ShapeDtypeStruct((NXI, TUBES), f32),
             jax.ShapeDtypeStruct((5, cells), f32),
         ),
-        in_specs=[
-            pl.BlockSpec(memory_space=pltpu.SMEM), vmem, pl.BlockSpec(memory_space=pl.ANY),
-            vmem, vmem, vmem, vmem,
-        ],
+        in_specs=[pl.BlockSpec(memory_space=pl.ANY)] * 7,
         out_specs=(pl.BlockSpec(memory_space=pl.ANY), vmem, vmem),
         scratch_shapes=[
+            pltpu.SMEM(row_table.shape, f32),
+            pltpu.VMEM(col_table.shape, f32),
+            pltpu.VMEM((1, cells), f32),
+            pltpu.VMEM((25, cells), f32),
+            pltpu.VMEM((25, cells), f32),
+            pltpu.VMEM((25, cells), f32),
+            dma((6,)),
             pltpu.VMEM((nodes, cells), f32),
             pltpu.VMEM((nodes, cells), f32),
             pltpu.VMEM((pairs, 24, TUBES), f32),
@@ -587,7 +618,7 @@
             dma((n_sec - 1,)), dma((n_sec - 1,)),
         ],
         compiler_params=pltpu.CompilerParams(
-            collective_id=0, has_side_effects=True, vmem_limit_bytes=40 * 1024 * 1024
+            collective_id=0, has_side_effects=True, vmem_limit_bytes=56 * 1024 * 1024
         ),
     )(
         jnp.asarray(row_table), jnp.asarray(col_table), distribution,

time: 69 us -> 70.2 us (1.017)
  Pallas kernels: 59.7 us -> 64.9 us
  local copies, waits for them, and re-layouts: 6.67 us -> 1.52 us
  other arithmetic: 1.5 us -> 2.99 us
    unnamed x15 -> x3, local copies, waits for them, and re-layouts: 6.46 us -> 0.6 us
    pallas_call x1, Pallas kernels: 59.7 us -> 64.9 us  [body(): pl.pallas_call(functools.partial(kernel, n_sec, n_vel, length, rows), out...]
    add x1, other arithmetic: 1.5 us -> 2.99 us  [body(): new = field + jnp.abs(field) * grow[None, :, 0:1]]
    slice x1, local copies, waits for them, and re-layouts: 0.11 us -> 0.82 us  [body(): new = field + jnp.abs(field) * grow[None, :, 0:1]]
where the time goes in v2:
time: 70.2 us; the launch traced here: 70 us
  Pallas kernels  64.9 us (92%)
  other arithmetic  2.99 us (4%)
  local copies, waits for them, and re-layouts  1.52 us (2%)
    pallas_call x1, Pallas kernels, body(): pl.pallas_call(functools.partial(kernel, n_sec, n_vel, length, rows), out...  64.9 us
    add x1, other arithmetic, body(): new = field + jnp.abs(field) * grow[None, :, 0:1]  2.99 us

profile of v2, /device:TPU:0, one launch (start us, length us, event | category | flops | bytes accessed | tf_op | source)
XLA Modules:
  0.0 70.0 jit_solution(10102231394815020522)
XLA Ops:
  0.6 64.9 %shard_map.86 = (f32[1728,256]{1,0:T(8,128)}, f32[24,128]{1,0:T(8,128)}, f32[5,256]{1,0:T(8,128)}) custom-call(f32[4032]{0:T(1024)} %constant.4.clone.table_in, f32[40,128]{1,0:T(8,128)} %constant.5.clone.cols_in, f32[1728,256]{1,0:T(8,128)} %dist.1, f32[1,256]{1,0:T(1,128)} %bitcast.1, f32[25,256]{1,0:T(8,128)} %lower_in.1, f32[25,256]{1,0:T(8,128)} %upper_in.1, ...), custom_call_target="tpu_custom_call" | custom-call | tf_op jit(solution)/shard_map/pallas_call | solution.py:573
  65.5 0.8 %slice_reduce_fusion = f32[24]{0:T(128)S(1)} fusion(f32[24,128]{1,0:T(8,128)} %get-tuple-element.6), kind=kLoop, calls=%fused_computation.1 | loop fusion | bytes 192 | tf_op jit(solution)/shard_map/slice | solution.py:628
  66.3 0.1 mul.17
  66.4 0.0 copy-start
  66.4 3.0 %multiply_add_fusion = f32[1728,256]{1,0:T(8,128)} fusion(f32[1728,256]{1,0:T(8,128)} %get-tuple-element.5, f32[1728]{0:T(1024)S(1)} %mul.17), kind=kLoop, calls=%fused_computation | loop fusion | flops 1327104 | bytes 3545856 | tf_op jit(solution)/shard_map/add | solution.py:628
  69.4 0.0 copy-done
  69.4 0.6 copy.10
  (1 shorter events, 0.0 us)
Async XLA Ops:
  66.4 3.0 %copy-start = (f32[5,256]{1,0:T(8,128)S(1)}, f32[5,256]{1,0:T(8,128)}, u32[]{:S(2)}) copy-start(f32[5,256]{1,0:T(8,128)} %get-tuple-element.11) | copy-start | bytes 15364

commit v3 on v2

--- a/solution.py
+++ b/solution.py
@@ -82,6 +82,7 @@
     dist_sem, syn_sem, p_send, p_recv, n_send, n_recv,
     a1_send, a1_recv, a2_send, a2_recv, a3_send, a3_recv,
     pb_send, pb_recv, b1_send, b1_recv, b2_send, b2_recv,
+    tmp_a, tmp_b, thr_own, thr_side, y_send, ta_recv, tb_recv, th_send, th_recv, px_send, px_recv,
 ):
     s = lax.axis_index("sec")
     v = lax.axis_index("vel")
@@ -191,6 +192,118 @@
         to = jnp.maximum(s - 1, 0)
         return remote(out_n.at[chunk(c)], in_n.at[chunk(c)], n_send.at[c], n_recv.at[c], {"sec": to})
 
+    square = n_sec == 4
+    outs, ins, thrs = (out_p, out_n), (in_p, in_n), (thr_p, thr_n)
+    x_sends, in_recvs = (p_send, n_send), (p_recv, n_recv)
+
+    def device_of(way, role):
+        return role if way == 0 else 3 - role
+
+    def when_role(way, role, run):
+        pl.when(s == device_of(way, role))(run)
+
+    def out_to(way, c, role):
+        return remote(outs[way].at[chunk(c)], ins[way].at[chunk(c)], x_sends[way].at[c],
+                      in_recvs[way].at[c], {"sec": device_of(way, role)})
+
+    def out_to_a(way, c, role):
+        return remote(outs[way].at[chunk(c)], tmp_a.at[way, chunk(c)], x_sends[way].at[c],
+                      ta_recv.at[way, c], {"sec": device_of(way, role)})
+
+    def out_to_b(way, c, role):
+        return remote(outs[way].at[chunk(c)], tmp_b.at[way, chunk(c)], x_sends[way].at[c],
+                      tb_recv.at[way, c], {"sec": device_of(way, role)})
+
+    def a_to(way, c, role):
+        return remote(tmp_a.at[way, chunk(c)], ins[way].at[chunk(c)], y_send.at[way, c],
+                      in_recvs[way].at[c], {"sec": device_of(way, role)})
+
+    def b_to(way, c, role):
+        return remote(tmp_b.at[way, chunk(c)], ins[way].at[chunk(c)], x_sends[way].at[c],
+                      in_recvs[way].at[c], {"sec": device_of(way, role)})
+
+    def thr_to(way, role):
+        return remote(thr_own.at[way], thr_side.at[way], th_send.at[way],
+                      th_recv.at[way], {"sec": device_of(way, role)})
+
+    if square:
+        for way in range(2):
+            thr_own[way] = thrs[way]
+            when_role(way, 1, lambda: thr_to(way, 0).start())
+            when_role(way, 2, lambda: thr_to(way, 3).start())
+
+    def launch(way, c):
+        when_role(way, 0, lambda: out_to(way, c, 1).start())
+        if c % 2 == 0:
+            when_role(way, 1, lambda: out_to_a(way, c, 0).start())
+        else:
+            when_role(way, 2, lambda: out_to_a(way, c, 3).start())
+
+    def near_job(way, i):
+        even, odd = 2 * i, 2 * i + 1
+
+        def role_0():
+            if i == 0:
+                thr_to(way, 1).wait_recv()
+            out_to_a(way, even, 1).wait_recv()
+            tmp_a[way, chunk(even)] = (
+                thr_side[way][None] * outs[way][chunk(even)] + tmp_a[way, chunk(even)]
+            )
+            a_to(way, even, 2).start()
+
+        def role_1():
+            out_to(way, odd, 0).wait_recv()
+            outs[way][chunk(odd)] = outs[way][chunk(odd)] + thrs[way][None] * ins[way][chunk(odd)]
+            out_to_b(way, odd, 3).start()
+
+        when_role(way, 0, role_0)
+        when_role(way, 1, role_1)
+
+    def far_job(way, i):
+        even, odd = 2 * i, 2 * i + 1
+
+        def role_2():
+            out_to(way, even, 3).wait_recv()
+            outs[way][chunk(even)] = outs[way][chunk(even)] + thrs[way][None] * ins[way][chunk(even)]
+            out_to(way, even, 3).start()
+
+        def role_3():
+            if i == 0:
+                thr_to(way, 2).wait_recv()
+            out_to_b(way, odd, 1).wait_recv()
+            b_to(way, odd, 2).start()
+            out_to_a(way, odd, 2).wait_recv()
+            ins[way][chunk(odd)] = (
+                thr_side[way][None] * tmp_b[way, chunk(odd)] + tmp_a[way, chunk(odd)]
+            )
+
+        when_role(way, 2, role_2)
+        when_role(way, 3, role_3)
+
+    def last_waits(way):
+        def even_in():
+            for c in range(0, CHUNKS, 2):
+                out_to(way, c, 2).wait_recv()
+
+        def odd_in():
+            for c in range(1, CHUNKS, 2):
+                out_to(way, c, 3).wait_recv()
+
+        when_role(way, 1, even_in)
+        when_role(way, 2, odd_in)
+        when_role(way, 3, even_in)
+
+    def sent(way, c):
+        when_role(way, 0, lambda: out_to(way, c, 1).wait_send())
+        if c % 2 == 0:
+            when_role(way, 0, lambda: a_to(way, c, 2).wait_send())
+            when_role(way, 1, lambda: out_to_a(way, c, 0).wait_send())
+            when_role(way, 2, lambda: out_to(way, c, 3).wait_send())
+        else:
+            when_role(way, 1, lambda: out_to_b(way, c, 3).wait_send())
+            when_role(way, 2, lambda: out_to_a(way, c, 3).wait_send())
+            when_role(way, 3, lambda: b_to(way, c, 2).wait_send())
+
     def first_pass(k, acc):
         acc = list(acc)
         bs = []
@@ -221,6 +334,10 @@
     acc = (zero,) * slices
     for c in range(CHUNKS):
         acc = lax.fori_loop(c * per, (c + 1) * per, first_pass, acc)
+        if square:
+            launch(0, c)
+            launch(1, c)
+            continue
 
         @pl.when(s == 0)
         def _():
@@ -256,16 +373,26 @@
             for e in range(25):
                 pb[pl.ds(base + k * 25 + e, 1), :] = block[e : e + 1, lanes]
         pb[pl.ds(base + 75, 1), :] = coll[0:1, lanes]
-    own = pl.ds(s * length * PROWS, length * PROWS)
+    core = lax.rem(v, 2)
+    share = length * PROWS // 2
+
+    def half_of(sec, which):
+        return pl.ds((sec * 2 + which) * share, share)
 
     def pb_copy(d):
         to = lax.rem(s + d, n_sec)
-        return remote(pb.at[own], pb.at[own], pb_send.at[d - 1], pb_recv.at[d - 1], {"sec": to})
+        mine_rows = pb.at[half_of(s, core)]
+        return remote(mine_rows, mine_rows, pb_send.at[d - 1], pb_recv.at[d - 1], {"sec": to})
 
     def pb_wait(d):
         frm = lax.rem(s + n_sec - d, n_sec)
-        there = pl.ds(frm * length * PROWS, length * PROWS)
-        remote(pb.at[there], pb.at[there], pb_send.at[d - 1], pb_recv.at[d - 1], {"sec": frm}).wait_recv()
+        there = pb.at[half_of(frm, core)]
+        remote(there, there, pb_send.at[d - 1], pb_recv.at[d - 1], {"sec": frm}).wait_recv()
+
+    def pb_cross(d, other=0):
+        frm = lax.rem(s + n_sec - d, n_sec)
+        there = pb.at[half_of(frm, core + other * (1 - 2 * core))]
+        return remote(there, there, px_send.at[d - 1], px_recv.at[d - 1], {"vel": v + 1 - 2 * core})
 
     for d in range(1, n_sec):
         pb_copy(d).start()
@@ -328,16 +455,33 @@
     when_owner(v, gather_slices)
     inner = jnp.logical_and(s > 0, s < n_sec - 1)
 
-    @pl.when(inner)
-    def _():
-        for c in range(CHUNKS):
-            relay(c)
-
+    if square:
+        steps = CHUNKS // 2
+
+        def jobs(first, second):
+            for i in range(steps + 1):
+                if i < steps:
+                    near_job(first, i)
+                if i > 0:
+                    far_job(second, i - 1)
+
+        pl.when(s < 2)(lambda: jobs(0, 1))
+        pl.when(s >= 2)(lambda: jobs(1, 0))
+    else:
+
+        @pl.when(inner)
+        def _():
+            for c in range(CHUNKS):
+                relay(c)
+
+    for d in range(1, n_sec):
+        pb_wait(d)
+        pb_cross(d).start()
     for d in range(1, n_vel):
         frm = lax.rem(v + n_vel - d, n_vel)
         when_owner(frm, lambda: a3(d, jnp.minimum(frm, slices - 1), frm).wait_recv())
     for d in range(1, n_sec):
-        pb_wait(d)
+        pb_cross(d, 1).wait_recv()
 
     hx, hxx, hxe = column(3), column(4), column(5)
     x2, en = column(1), column(2)
@@ -442,10 +586,15 @@
         t_loc[p * 4 + 2] = t_all[2 * total + at] + 2.0 * c[3]
         t_loc[p * 4 + 3] = t_all[3 * total + at] + c[4] * (1.0 / 1.5)
 
-    @pl.when(jnp.logical_not(inner))
-    def _():
-        for c in range(CHUNKS):
-            relay(c)
+    if square:
+        last_waits(0)
+        last_waits(1)
+    else:
+
+        @pl.when(jnp.logical_not(inner))
+        def _():
+            for c in range(CHUNKS):
+                relay(c)
 
     def second_pass(k, acc):
         n_mix, p_mix = in_n[k, 16:24], in_p[k, 16:24]
@@ -538,8 +687,16 @@
         shift_mass = new_mass
     grow_out[...] = jnp.exp(shift_mass + shift_flow * column(6)) - 1.0
 
+    if square:
+        for way in range(2):
+            when_role(way, 1, lambda: thr_to(way, 0).wait_send())
+            when_role(way, 2, lambda: thr_to(way, 3).wait_send())
     for c in range(CHUNKS):
         stores[c].wait()
+        if square:
+            sent(0, c)
+            sent(1, c)
+            continue
 
         @pl.when(s < n_sec - 1)
         def _():
@@ -555,6 +712,7 @@
         b1[d - 1].wait_send()
     for d in range(1, n_sec):
         pb_copy(d).wait_send()
+        pb_cross(d).wait_send()
         when_owner(v, lambda: a2(d, s, lax.rem(s + d, n_sec)).wait_send())
         b2[d - 1].wait_send()
 
@@ -616,6 +774,12 @@
             dma((n_sec - 1,)), dma((n_sec - 1,)),
             dma((n_vel - 1,)), dma((n_vel - 1,)),
             dma((n_sec - 1,)), dma((n_sec - 1,)),
+            pltpu.VMEM((2, pairs, 24, TUBES), f32),
+            pltpu.VMEM((2, pairs, 24, TUBES), f32),
+            pltpu.VMEM((2, 24, TUBES), f32),
+            pltpu.VMEM((2, 24, TUBES), f32),
+            dma((2, CHUNKS)), dma((2, CHUNKS)), dma((2, CHUNKS)), dma((2,)), dma((2,)),
+            dma((n_sec - 1,)), dma((n_sec - 1,)),
         ],
         compiler_params=pltpu.CompilerParams(
             collective_id=0, has_side_effects=True, vmem_limit_bytes=56 * 1024 * 1024

time: 70.2 us -> 45.6 us (0.65)
  Pallas kernels: 64.9 us -> 40.2 us
    pallas_call x1, Pallas kernels: 64.9 us -> 40.2 us  [body(): pl.pallas_call(functools.partial(kernel, n_sec, n_vel, length, rows), out...]
where the time goes in v3:
time: 45.6 us; the launch traced here: 45.3 us
  Pallas kernels  40.2 us (88%)
  other arithmetic  2.99 us (7%)
  local copies, waits for them, and re-layouts  1.52 us (3%)
  between operations  0.66 us (1%)
    pallas_call x1, Pallas kernels, body(): pl.pallas_call(functools.partial(kernel, n_sec, n_vel, length, rows), out...  40.2 us
    add x1, other arithmetic, body(): new = field + jnp.abs(field) * grow[None, :, 0:1]  2.99 us

profile of v3, /device:TPU:0, one launch (start us, length us, event | category | flops | bytes accessed | tf_op | source)
XLA Modules:
  0.0 45.3 jit_solution(5429661665233290428)
XLA Ops:
  0.6 40.2 %shard_map.86 = (f32[1728,256]{1,0:T(8,128)}, f32[24,128]{1,0:T(8,128)}, f32[5,256]{1,0:T(8,128)}) custom-call(f32[4032]{0:T(1024)} %constant.4.clone.table_in, f32[40,128]{1,0:T(8,128)} %constant.5.clone.cols_in, f32[1728,256]{1,0:T(8,128)} %dist.1, f32[1,256]{1,0:T(1,128)} %bitcast.1, f32[25,256]{1,0:T(8,128)} %lower_in.1, f32[25,256]{1,0:T(8,128)} %upper_in.1, ...), custom_call_target="tpu_custom_call" | custom-call | tf_op jit(solution)/shard_map/pallas_call | solution.py:731
  40.8 0.8 %slice_reduce_fusion = f32[24]{0:T(128)S(1)} fusion(f32[24,128]{1,0:T(8,128)} %get-tuple-element.6), kind=kLoop, calls=%fused_computation.1 | loop fusion | bytes 192 | tf_op jit(solution)/shard_map/slice | solution.py:792
  41.6 0.1 mul.17
  41.7 0.0 copy-start
  41.7 3.0 %multiply_add_fusion = f32[1728,256]{1,0:T(8,128)} fusion(f32[1728,256]{1,0:T(8,128)} %get-tuple-element.5, f32[1728]{0:T(1024)S(1)} %mul.17), kind=kLoop, calls=%fused_computation | loop fusion | flops 1327104 | bytes 3545856 | tf_op jit(solution)/shard_map/add | solution.py:792
  44.7 0.0 copy-done
  44.7 0.6 %copy.10 = f32[5,256]{1,0:T(8,128)} copy(f32[5,256]{1,0:T(8,128)S(1)} %copy-done) | data formatting | bytes 10240
  (1 shorter events, 0.0 us)
Async XLA Ops:
  41.7 3.0 %copy-start = (f32[5,256]{1,0:T(8,128)S(1)}, f32[5,256]{1,0:T(8,128)}, u32[]{:S(2)}) copy-start(f32[5,256]{1,0:T(8,128)} %get-tuple-element.11) | copy-start | bytes 15364

commit v4 on v3

--- a/solution.py
+++ b/solution.py
@@ -13,7 +13,6 @@
 TUBES = 128
 JACOBI = 4
 NEWTON = 2
-CHUNKS = 6
 PROWS = 80
 pseudo_rate = 1.0
 MESH = pl.DeviceIdType.MESH
@@ -72,6 +71,10 @@
     return rows, cols.astype(np.float32)
 
 
+def chunks_of(pairs):
+    return 12 if pairs % 12 == 0 else 6
+
+
 def kernel(
     n_sec, n_vel, length, rows,
     table_in, cols_in, dist, coll_in, lower_in, upper_in, diag_in,
@@ -89,7 +92,8 @@
     total = n_sec * length
     slices = 4 * length
     pairs = rows // 2
-    per = pairs // CHUNKS
+    chunks = chunks_of(pairs)
+    per = pairs // chunks
     all_rows = NXI * NXI
 
     load = pltpu.make_async_copy(dist, dv, dist_sem)
@@ -233,10 +237,10 @@
             when_role(way, 2, lambda: thr_to(way, 3).start())
 
     def launch(way, c):
-        when_role(way, 0, lambda: out_to(way, c, 1).start())
         if c % 2 == 0:
             when_role(way, 1, lambda: out_to_a(way, c, 0).start())
         else:
+            when_role(way, 0, lambda: out_to(way, c, 1).start())
             when_role(way, 2, lambda: out_to_a(way, c, 3).start())
 
     def near_job(way, i):
@@ -280,18 +284,12 @@
         when_role(way, 2, role_2)
         when_role(way, 3, role_3)
 
-    def last_waits(way):
-        def even_in():
-            for c in range(0, CHUNKS, 2):
-                out_to(way, c, 2).wait_recv()
-
-        def odd_in():
-            for c in range(1, CHUNKS, 2):
-                out_to(way, c, 3).wait_recv()
-
-        when_role(way, 1, even_in)
-        when_role(way, 2, odd_in)
-        when_role(way, 3, even_in)
+    def last_wait(way, c):
+        if c % 2 == 0:
+            when_role(way, 1, lambda: out_to(way, c, 2).wait_recv())
+            when_role(way, 3, lambda: out_to(way, c, 2).wait_recv())
+        else:
+            when_role(way, 2, lambda: out_to(way, c, 3).wait_recv())
 
     def sent(way, c):
         when_role(way, 0, lambda: out_to(way, c, 1).wait_send())
@@ -332,7 +330,7 @@
         return tuple(acc)
 
     acc = (zero,) * slices
-    for c in range(CHUNKS):
+    for c in range(chunks):
         acc = lax.fori_loop(c * per, (c + 1) * per, first_pass, acc)
         if square:
             launch(0, c)
@@ -394,8 +392,6 @@
         there = pb.at[half_of(frm, core + other * (1 - 2 * core))]
         return remote(there, there, px_send.at[d - 1], px_recv.at[d - 1], {"vel": v + 1 - 2 * core})
 
-    for d in range(1, n_sec):
-        pb_copy(d).start()
 
     mine = jnp.minimum(v, slices - 1)
 
@@ -413,7 +409,14 @@
         for d in range(1, n_sec):
             a2(d, s, lax.rem(s + d, n_sec)).start()
 
+
     when_owner(v, reduce_slices)
+    if square:
+        for c in range(0, chunks, 2):
+            when_role(0, 0, lambda: out_to(0, c, 1).start())
+            when_role(1, 0, lambda: out_to(1, c, 1).start())
+    for d in range(1, n_sec):
+        pb_copy(d).start()
 
     def relay(c):
         def forward_pos():
@@ -452,15 +455,18 @@
         for d in range(1, n_vel):
             a3(d, mine, lax.rem(v + d, n_vel)).start()
 
+    if square:
+        pl.when(s < 2)(lambda: near_job(0, 0))
+        pl.when(s >= 2)(lambda: near_job(1, 0))
     when_owner(v, gather_slices)
     inner = jnp.logical_and(s > 0, s < n_sec - 1)
 
     if square:
-        steps = CHUNKS // 2
+        steps = chunks // 2
 
         def jobs(first, second):
             for i in range(steps + 1):
-                if i < steps:
+                if 0 < i < steps:
                     near_job(first, i)
                 if i > 0:
                     far_job(second, i - 1)
@@ -471,7 +477,7 @@
 
         @pl.when(inner)
         def _():
-            for c in range(CHUNKS):
+            for c in range(chunks):
                 relay(c)
 
     for d in range(1, n_sec):
@@ -586,14 +592,11 @@
         t_loc[p * 4 + 2] = t_all[2 * total + at] + 2.0 * c[3]
         t_loc[p * 4 + 3] = t_all[3 * total + at] + c[4] * (1.0 / 1.5)
 
-    if square:
-        last_waits(0)
-        last_waits(1)
-    else:
+    if not square:
 
         @pl.when(jnp.logical_not(inner))
         def _():
-            for c in range(CHUNKS):
+            for c in range(chunks):
                 relay(c)
 
     def second_pass(k, acc):
@@ -627,7 +630,10 @@
 
     acc = zero
     stores = []
-    for c in range(CHUNKS):
+    for c in range(chunks):
+        if square:
+            last_wait(0, c)
+            last_wait(1, c)
         acc = lax.fori_loop(c * per, (c + 1) * per, second_pass, acc)
         part = pl.ds(c * per * 48, per * 48)
         store = pltpu.make_async_copy(syn.at[part], syn_out.at[part], syn_sem.at[c])
@@ -685,13 +691,15 @@
         new_mass = shift_mass - (m2 * miss_mass - m1 * miss_flow) / determinant
         shift_flow = shift_flow - (m0 * miss_flow - m1 * miss_mass) / determinant
         shift_mass = new_mass
-    grow_out[...] = jnp.exp(shift_mass + shift_flow * column(6)) - 1.0
+    grown = jnp.exp(shift_mass + shift_flow * column(6)) - 1.0
+    for p in range(length):
+        grow_out[:, p * TUBES : (p + 1) * TUBES] = grown
 
     if square:
         for way in range(2):
             when_role(way, 1, lambda: thr_to(way, 0).wait_send())
             when_role(way, 2, lambda: thr_to(way, 3).wait_send())
-    for c in range(CHUNKS):
+    for c in range(chunks):
         stores[c].wait()
         if square:
             sent(0, c)
@@ -723,6 +731,7 @@
     rows = nodes // NXI
     pairs = rows // 2
     slices = 4 * length
+    chunks = chunks_of(pairs)
     total = n_sec * length
     row_table, col_table = tables()
     f32 = jnp.float32
@@ -732,7 +741,7 @@
         functools.partial(kernel, n_sec, n_vel, length, rows),
         out_shape=(
             jax.ShapeDtypeStruct((nodes, cells), f32),
-            jax.ShapeDtypeStruct((NXI, TUBES), f32),
+            jax.ShapeDtypeStruct((NXI, cells), f32),
             jax.ShapeDtypeStruct((5, cells), f32),
         ),
         in_specs=[pl.BlockSpec(memory_space=pl.ANY)] * 7,
@@ -767,7 +776,7 @@
             pltpu.VMEM((n_vel - 1, 8, TUBES), f32),
             pltpu.VMEM((n_sec - 1, 8, TUBES), f32),
             dma,
-            dma((CHUNKS,)), dma((CHUNKS,)), dma((CHUNKS,)), dma((CHUNKS,)), dma((CHUNKS,)),
+            dma((chunks,)), dma((chunks,)), dma((chunks,)), dma((chunks,)), dma((chunks,)),
             dma((n_vel - 1,)), dma((n_vel - 1,)),
             dma((n_sec - 1,)), dma((n_sec - 1,)),
             dma((n_vel - 1,)), dma((n_vel - 1,)),
@@ -778,7 +787,7 @@
             pltpu.VMEM((2, pairs, 24, TUBES), f32),
             pltpu.VMEM((2, 24, TUBES), f32),
             pltpu.VMEM((2, 24, TUBES), f32),
-            dma((2, CHUNKS)), dma((2, CHUNKS)), dma((2, CHUNKS)), dma((2,)), dma((2,)),
+            dma((2, chunks)), dma((2, chunks)), dma((2, chunks)), dma((2,)), dma((2,)),
             dma((n_sec - 1,)), dma((n_sec - 1,)),
         ],
         compiler_params=pltpu.CompilerParams(
@@ -789,7 +798,7 @@
         collision.reshape(1, cells), lower_blocks, upper_blocks, diag_inverse,
     )
     field = syn.reshape(rows, NXI, cells)
-    new = field + jnp.abs(field) * grow[None, :, 0:1]
+    new = field + jnp.abs(field) * grow[None]
     return (new.reshape(nodes, cells), macro)
 
 

time: 45.6 us -> 44.6 us (0.978)
  local copies, waits for them, and re-layouts: 1.52 us -> 0.6 us
    slice x1 -> x0, local copies, waits for them, and re-layouts: 0.82 us -> none  [body(): new = field + jnp.abs(field) * grow[None, :, 0:1]]
where the time goes in v4:
time: 44.6 us; the launch traced here: 44.4 us
  Pallas kernels  40.3 us (90%)
  other arithmetic  2.87 us (6%)
  between operations  0.65 us (1%)
  local copies, waits for them, and re-layouts  0.6 us (1%)
    pallas_call x1, Pallas kernels, body(): pl.pallas_call(functools.partial(kernel, n_sec, n_vel, length, rows), out...  40.3 us
    add x1, other arithmetic, body(): new = field + jnp.abs(field) * grow[None]  2.87 us

profile of v4, /device:TPU:0, one launch (start us, length us, event | category | flops | bytes accessed | tf_op | source)
XLA Modules:
  0.0 44.4 jit_solution(11201835733576897127)
XLA Ops:
  0.6 40.3 %shard_map.86 = (f32[1728,256]{1,0:T(8,128)}, f32[24,256]{1,0:T(8,128)}, f32[5,256]{1,0:T(8,128)}) custom-call(f32[4032]{0:T(1024)} %constant.4.clone.table_in, f32[40,128]{1,0:T(8,128)} %constant.5.clone.cols_in, f32[1728,256]{1,0:T(8,128)} %dist.1, f32[1,256]{1,0:T(1,128)} %bitcast.5, f32[25,256]{1,0:T(8,128)} %lower_in.1, f32[25,256]{1,0:T(8,128)} %upper_in.1, ...), custom_call_target="tpu_custom_call" | custom-call | tf_op jit(solution)/shard_map/pallas_call | solution.py:740
  40.9 0.0 copy-start
  40.9 2.9 %fusion = f32[1728,256]{1,0:T(8,128)} fusion(f32[1728,256]{1,0:T(8,128)} %get-tuple-element.5, f32[24,256]{1,0:T(8,128)} %get-tuple-element.6), kind=kLoop, calls=%fused_computation.1 | loop fusion | flops 1327104 | bytes 3563520 | tf_op jit(solution)/shard_map/add | solution.py:801
  43.8 0.0 copy-done
  43.8 0.6 %copy.10 = f32[5,256]{1,0:T(8,128)} copy(f32[5,256]{1,0:T(8,128)S(1)} %copy-done) | data formatting | bytes 10240
Async XLA Ops:
  40.9 2.9 %copy-start = (f32[5,256]{1,0:T(8,128)S(1)}, f32[5,256]{1,0:T(8,128)}, u32[]{:S(2)}) copy-start(f32[5,256]{1,0:T(8,128)} %get-tuple-element.11) | copy-start | bytes 15364
